TPU v7x, 256 devices: a whole 4x4x8 slice. The times are simulated.
256 devices in a mesh: dp: 32 (over x, y, core), proto: 8 (over z).
Axes of the slice: x: 4, y: 4, z: 8, core: 2. Of those that a mesh axis runs over, the one named last changes fastest.
Arguments:
- teacher_feats: bfloat16 [8192, 256], P('dp'), may hold values from -4 to 4
- student_feats: bfloat16 [8192, 256], P('dp'), may hold values from -4 to 4
- proto_weight: bfloat16 [256, 65536], P(None, 'proto'), may hold values from -1 to 1
- token_mask: int32 [8192], P('dp'), may hold values 0 or 1
Outputs:
- targets: bfloat16 [8192, 65536], P('dp', 'proto')
- weight_grad: float32 [256, 65536], P('dp', 'proto')
- feature_grad: float32 [8192, 256], P('dp', 'proto')
All inputs are finite; a program needn't handle non-finite values. No bound on the sum of `token_mask` on one device may be relied on, other than what follows from the above.
Results may differ from a plain program's by a relative error of at most 0.0029.
Values sent between devices are 32-bit elements; how exact they have to be, the bound alone decides.
A program may use at most 128 MiB of HBM per device.

v0:
```python
import jax
import jax.numpy as jnp
from jax import lax
from jax.sharding import PartitionSpec as P

SWEEPS = 3


teacher_temp = 0.07
student_temp = 0.1


def on_device(teacher_feats, student_feats, proto_weight, token_mask):
    live_rows = token_mask.astype(jnp.float32)
    teacher_logits = (
        jnp.dot(teacher_feats, proto_weight, preferred_element_type=jnp.float32) / teacher_temp
    )
    row_peak = lax.pmax(jnp.max(teacher_logits, axis=1), "proto")
    expo_table = live_rows[:, None] * jnp.exp(teacher_logits - row_peak[:, None])
    target = expo_table
    for sweep_index in range(SWEEPS):
        column_total = lax.psum(jnp.sum(target, axis=0), "dp")
        target = target / column_total[None, :]
        row_total = lax.psum(jnp.sum(target, axis=1), "proto")
        target = target / (row_total + 1.0 - live_rows)[:, None]
    student_logits = (
        jnp.dot(student_feats, proto_weight, preferred_element_type=jnp.float32) / student_temp
    )
    local_peak = jnp.max(student_logits, axis=1)
    joint_peak = lax.pmax(local_peak, "proto")
    local_total = jnp.sum(jnp.exp(student_logits - joint_peak[:, None]), axis=1)
    joint_total = lax.psum(local_total, "proto")
    lse_rows = joint_peak + jnp.log(joint_total)
    delta = (live_rows[:, None] * (jnp.exp(student_logits - lse_rows[:, None]) - target)).astype(
        jnp.bfloat16
    )
    feature_part = lax.dot_general(
        delta, proto_weight, (((1,), (1,)), ((), ())), preferred_element_type=jnp.float32
    )
    feature_grad = lax.psum_scatter(feature_part, "proto", scatter_dimension=1, tiled=True)
    weight_grad = lax.psum_scatter(
        lax.dot_general(
            student_feats, delta, (((0,), (0,)), ((), ())), preferred_element_type=jnp.float32
        ),
        "dp",
        scatter_dimension=0,
        tiled=True,
    )
    return (target.astype(jnp.bfloat16), weight_grad, feature_grad)


def solution(mesh):
    placed = (P("dp", None), P("dp", None), P(None, "proto"), P("dp"))
    return jax.shard_map(
        on_device,
        mesh=mesh,
        in_specs=placed,
        out_specs=(P("dp", "proto"), P("dp", "proto"), P("dp", "proto")),
        check_vma=False,
    )
```

profile of v0, /device:TPU:1, one launch (start us, length us, event | category | flops | bytes accessed | tf_op | source)
XLA Modules:
  0.0 648.1 jit_solution(556137975122501962)
XLA Ops:
  7.2 0.0 copy-start
  7.2 0.0 reduce-scatter.5.cloned.1.call-start
  7.2 0.0 copy-start.2
  7.2 0.8 convert_element_type.9
  8.1 7.0 %fusion.13 = (f32[256]{0:T(256)S(1)}, f32[256,8192]{1,0:T(8,128)}) fusion(bf16[256,256]{1,0:T(8,128)(2,1)} %param.4, bf16[256,8192]{1,0:T(8,128)(2,1)} %param.6), kind=kOutput, calls=%fused_computation.26 | convolution fusion | flops 1077935872 | bytes 12715008 | tf_op jit(solution)/shard_map/dot_general | solution.py:16
  15.1 0.0 copy-done
  15.1 0.0 copy-done.2
  15.1 4.5 fusion.14
  19.6 17.3 %all-reduce.1 = (f32[256]{0:T(256)S(1)}, f32[256]{0:T(256)S(1)}) all-reduce(f32[256]{0:T(256)S(1)} %get-tuple-element.15, f32[256]{0:T(256)S(1)} %get-tuple-element.17), channel_id=1, replica_groups=mesh['dp'=32,'proto'=8] {'proto'}, use_global_device_ids=true, to_apply=%region_1.0 | all-reduce | flops 512 | bytes 4096 | tf_op jit(solution)/shard_map/pmax | solution.py:18
  36.9 5.0 fusion.12
  41.9 123.4 %psum.49 = f32[8192]{0:T(1024)S(1)} all-reduce(f32[8192]{0:T(1024)S(1)} %fusion.12), channel_id=1, replica_groups=mesh['dp'=32,'proto'=8] {'dp'}, use_global_device_ids=true, to_apply=%region_3.0 | all-reduce | flops 8192 | bytes 65536 | tf_op jit(solution)/shard_map/psum | solution.py:22
  165.3 4.5 divide_reduce_fusion
  169.8 10.7 %psum.50 = f32[256]{0:T(256)S(1)} all-reduce(f32[256]{0:T(256)S(1)} %divide_reduce_fusion), channel_id=1, replica_groups=mesh['dp'=32,'proto'=8] {'proto'}, use_global_device_ids=true, to_apply=%region_5.0 | all-reduce | flops 256 | bytes 2048 | tf_op jit(solution)/shard_map/psum | solution.py:24
  180.5 5.6 fusion.7
  186.1 127.2 %psum.51 = f32[8192]{0:T(1024)S(1)} all-reduce(f32[8192]{0:T(1024)S(1)} %fusion.7), channel_id=1, replica_groups=mesh['dp'=32,'proto'=8] {'dp'}, use_global_device_ids=true, to_apply=%region_7.0 | all-reduce | flops 8192 | bytes 65536 | tf_op jit(solution)/shard_map/psum | solution.py:22
  313.3 4.9 fusion.8
  318.3 12.4 %psum.52 = f32[256]{0:T(256)S(1)} all-reduce(f32[256]{0:T(256)S(1)} %fusion.8), channel_id=1, replica_groups=mesh['dp'=32,'proto'=8] {'proto'}, use_global_device_ids=true, to_apply=%region_9.0 | all-reduce | flops 256 | bytes 2048 | tf_op jit(solution)/shard_map/psum | solution.py:24
  330.7 5.4 fusion.9
  336.1 127.7 %psum.53 = f32[8192]{0:T(1024)S(1)} all-reduce(f32[8192]{0:T(1024)S(1)} %fusion.9), channel_id=1, replica_groups=mesh['dp'=32,'proto'=8] {'dp'}, use_global_device_ids=true, to_apply=%region_11.0 | all-reduce | flops 8192 | bytes 65536 | tf_op jit(solution)/shard_map/psum | solution.py:22
  463.8 5.7 fusion.10
  469.5 4.6 exponential_reduce_fusion
  474.1 10.7 %all-reduce = (f32[256]{0:T(256)S(1)}, f32[256]{0:T(256)S(1)}) all-reduce(f32[256]{0:T(256)S(1)} %fusion.10, f32[256]{0:T(256)S(1)} %exponential_reduce_fusion), channel_id=1, replica_groups=mesh['dp'=32,'proto'=8] {'proto'}, use_global_device_ids=true, to_apply=%region_13.0 | all-reduce | flops 512 | bytes 4096 | tf_op jit(solution)/shard_map/psum | solution.py:24
  484.8 10.6 %multiply_convert_fusion = (bf16[256,8192]{1,0:T(8,128)(2,1)S(1)}, bf16[256,8192]{1,0:T(8,128)(2,1)}) fusion(f32[256,8192]{1,0:T(8,128)} %get-tuple-element.18, f32[256]{0:T(256)S(1)} %get-tuple-element.19, f32[256]{0:T(256)S(1)} %convert_element_type.9, f32[256]{0:T(256)S(1)} %get-tuple-element.20, f32[8192]{0:T(1024)S(1)} %psum.53, ...), kind=kLoop, calls=%fused_computation.12 | loop fusion | flops 27262976 | bytes 25270272 | tf_op jit(solution)/shard_map/convert_element_type | solution.py:34
  495.4 2.0 copy-done.1
  497.4 2.0 fusion.15
  499.4 0.0 reduce-scatter.5.cloned.1.call-update
  499.4 0.0 reduce-scatter.7.cloned.1.call-start
  499.5 6.7 %convolution_bitcast_fusion = f32[256,8192]{0,1:T(8,128)} fusion(bf16[256,8192]{1,0:T(8,128)(2,1)} %copy-done.1, bf16[256,256]{1,0:T(8,128)(2,1)S(1)} %copy-done), kind=kOutput, calls=%fused_computation.6 | convolution fusion | flops 1073741824 | bytes 12713984 | tf_op jit(solution)/shard_map/dot_general | solution.py:42
  506.2 8.9 %copy.9 = f32[256,8192]{1,0:T(8,128)} copy(f32[256,8192]{0,1:T(8,128)} %convolution_bitcast_fusion) | data formatting | bytes 16777216
  515.1 0.0 reduce-scatter.7.cloned.1.call-update
  515.1 18.2 %reduce-scatter.5.cloned.1.call-done = f32[256,32]{0,1:T(8,128)} async-done(((f32[256,256]{0,1:T(8,128)}), f32[256,32]{0,1:T(8,128)}) %reduce-scatter.5.cloned.1.call-update) | async-done | bytes 32784 | tf_op jit(solution)/shard_map/reduce_scatter | solution.py:40
  533.3 108.0 %reduce-scatter.7.cloned.1.call-done = f32[8,8192]{1,0:T(8,128)} async-done(((f32[256,8192]{1,0:T(8,128)}), f32[8,8192]{1,0:T(8,128)}) %reduce-scatter.7.cloned.1.call-update) | async-done | bytes 262160
  (8 shorter events, 0.0 us)
Async XLA Ops:
  7.2 7.9 %copy-start = (bf16[256,256]{1,0:T(8,128)(2,1)S(1)}, bf16[256,256]{1,0:T(8,128)(2,1)}, u32[]{:S(2)}) copy-start(bf16[256,256]{1,0:T(8,128)(2,1)} %param.5) | copy-start | bytes 393220
  7.2 526.1 %reduce-scatter.5.cloned.1.call-start = ((), (), s32[]{:S(2)}) async-start(), calls=%async_computation.2 | async-start | bytes 294912 | tf_op jit(solution)/shard_map/reduce_scatter | solution.py:40
  7.2 7.9 %copy-start.2 = (bf16[256,8192]{1,0:T(8,128)(2,1)S(1)}, bf16[256,8192]{1,0:T(8,128)(2,1)}, u32[]{:S(2)}) copy-start(bf16[256,8192]{1,0:T(8,128)(2,1)} %param.6) | copy-start | bytes 12582916
  36.9 143.6 %copy-start.4 = (s32[256]{0:T(256)S(1)}, s32[256]{0:T(256)}, u32[]{:S(2)}) copy-start(s32[256]{0:T(256)} %param.7) | copy-start | bytes 3076
  484.8 12.6 %copy-start.3 = (bf16[256,8192]{1,0:T(8,128)(2,1)S(1)}, bf16[256,8192]{1,0:T(8,128)(2,1)}, u32[]{:S(2)}) copy-start(bf16[256,8192]{1,0:T(8,128)(2,1)} %param.6) | copy-start | bytes 12582916
  495.4 2.0 copy-start.1
  499.4 141.9 %reduce-scatter.7.cloned.1.call-start = ((), (), s32[]{:S(2)}) async-start(), calls=%async_computation.3 | async-start | bytes 8650752
Sparse Core Ops, SparseCore 0:
  499.5 33.7 reduce-scatter.4
  538.4 102.8 reduce-scatter.6
where the time goes:
time: 649 us; the launch traced here: 648 us
  blocking collectives  429 us (66%)
  waiting for transfers between devices  126 us (19%)
  other arithmetic  47.2 us (7%)
  matrix products  20.3 us (3%)
  between operations  14.1 us (2%)
  local copies, waits for them, and re-layouts  10.9 us (2%)
    psum x3, blocking collectives, on_device(): column_total = lax.psum(jnp.sum(target, axis=0), 'dp')  378 us
    unnamed x3, waiting for transfers between devices  108 us
    psum x3, blocking collectives, on_device(): row_total = lax.psum(jnp.sum(target, axis=1), 'proto')  33.8 us
    reduce_scatter x1, waiting for transfers between devices, on_device(): lax.psum_scatter(feature_part, 'proto', scatter_dimension=1, tiled=True)  18.2 us
    pmax x1, blocking collectives, on_device(): row_peak = lax.pmax(jnp.max(teacher_logits, axis=1), 'proto')  17.3 us
    reduce_sum x3, other arithmetic, on_device(): column_total = lax.psum(jnp.sum(target, axis=0), 'dp')  16 us
    reduce_sum x3, other arithmetic, on_device(): row_total = lax.psum(jnp.sum(target, axis=1), 'proto')  15.1 us
  transfers between devices with their start and end apart: 2, of which 2 were waited for; matrix products, arithmetic and copies ran while one was open for 2% of the time, Pallas kernels for 0%

commit v1 on v0

v1 whole, which is shorter than its diff:
```python
import math

import jax
import jax.numpy as jnp
from jax import lax
from jax.experimental import pallas as pl
from jax.experimental.pallas import tpu as pltpu
from jax.sharding import PartitionSpec as P

SWEEPS = 3
TEACHER = math.log2(math.e) / 0.07
STUDENT = math.log2(math.e) / 0.1
MESH = pl.DeviceIdType.MESH
NX, NY, NC, NZ = 4, 4, 2, 8
ROWS = 256
WIDE = 1024
BLOCKS = 8
TILES = WIDE // 128


def wait_all(ref, sem):
    pltpu.make_async_copy(ref, ref, sem).wait()


def to_rows(lanes):
    return jnp.transpose(jnp.broadcast_to(lanes, (128, ROWS)))


def kernel(
    tf_ref, sf_ref, mask_ref, w_hbm,
    out_hbm, weight_hbm, feature_ref,
    w, expo, soft, peak_b, acc, t_b, g_b, sft, tgt, wpart,
    col_tx, core_rx, x_tx, x_rx, y_tx, y_rx, p_ref,
    z_tx, z_rx, s_tx, s_rx,
    w_sem, out_sem, send, recv,
):
    dp = lax.axis_index("dp")
    z = lax.axis_index("proto")
    cx, cy, cc = dp // (NY * NC), lax.rem(dp // NC, NY), lax.rem(dp, NC)

    def at(x, y, c):
        return {"dp": (x * NY + y) * NC + c}

    partner = at(cx, cy, 1 - cc)
    x_peers = [at(lax.rem(cx + k, NX), cy, cc) for k in range(1, NX)]
    y_peers = [at(cx, lax.rem(cy + k, NY), cc) for k in range(1, NY)]
    z_peers = [{"proto": lax.rem(z + k, NZ)} for k in range(1, NZ)]

    barrier = pltpu.get_barrier_semaphore()
    peers = [partner] + x_peers + y_peers + z_peers
    for peer in peers:
        pl.semaphore_signal(barrier, inc=1, device_id=peer, device_id_type=MESH)

    def load(b):
        return pltpu.make_async_copy(
            w_hbm.at[:, pl.ds(pl.multiple_of(b * WIDE, WIDE), WIDE)], w.at[b], w_sem.at[b]
        )

    def start_load(b, c):
        load(b).start()
        return c

    lax.fori_loop(0, BLOCKS, start_load, 0)

    def push(src, dst, group, devices):
        for k, device in enumerate(devices):
            pltpu.make_async_remote_copy(
                src_ref=src, dst_ref=dst.at[k], send_sem=send.at[group], recv_sem=recv.at[group],
                device_id=device, device_id_type=MESH,
            ).start()

    def logits(feats_ref, table, first):
        acc[...] = jnp.full(acc.shape, -jnp.inf, jnp.float32)

        def block(b, c):
            if first:
                load(b).wait()
            for s in range(WIDE // 256):
                part = jnp.dot(
                    feats_ref[...], w[b, :, s * 256:(s + 1) * 256],
                    preferred_element_type=jnp.float32,
                )
                table[b, :, s * 256:(s + 1) * 256] = part
                acc[...] = jnp.maximum(acc[...], jnp.maximum(part[:, :128], part[:, 128:]))
            return c

        lax.fori_loop(0, BLOCKS, block, 0)
        peak_b[...] = jnp.broadcast_to(jnp.max(acc[...], axis=1, keepdims=True), acc.shape)
        return jnp.max(jnp.transpose(acc[...]), axis=0, keepdims=True)

    def powers(table, scale, low, high, total):
        def block(b, c):
            for s in range(TILES):
                at_s = (b, slice(None), slice(s * 128, (s + 1) * 128))
                value = jnp.exp2((table[at_s] - peak_b[...]) * scale)
                table[at_s] = value
                if total:
                    acc[...] += value
            return c

        lax.fori_loop(low, high, block, 0)

    def row_sum():
        return jnp.sum(jnp.transpose(acc[...]), axis=0, keepdims=True)

    live = mask_ref[...].astype(jnp.float32)

    local_peak = logits(tf_ref, expo, True)
    z_tx[0] = local_peak
    pl.semaphore_wait(barrier, len(peers))
    push(z_tx.at[0], z_rx.at[0], 0, z_peers)
    powers(expo, TEACHER, 0, BLOCKS, False)
    sft[...] = jnp.transpose(sf_ref[...])
    wait_all(z_rx.at[0], recv.at[0])
    joint_peak = jnp.maximum(jnp.max(z_rx[0], axis=0), local_peak)
    factor = live * jnp.exp2((local_peak - joint_peak) * TEACHER)
    t_b[...] = to_rows(factor)

    for sweep in range(SWEEPS):
        base = 2 + 5 * sweep

        def column_block(b, c):
            for s in range(TILES):
                col = expo[b, :, s * 128:(s + 1) * 128] * t_b[...]
                col_tx[pl.ds(b * TILES + s, 1), :] = jnp.sum(col, axis=0, keepdims=True)
            return c

        lax.fori_loop(0, BLOCKS, column_block, 0)
        half = BLOCKS * TILES // 2
        mine = pl.ds(pl.multiple_of(cc * half, half), half)
        other = pl.ds(pl.multiple_of((1 - cc) * half, half), half)
        push(col_tx.at[other], core_rx.at[sweep], base, [partner])
        wait_all(core_rx.at[sweep], recv.at[base])
        x_sum = col_tx[mine, :] + core_rx[sweep, 0]
        x_tx[sweep] = x_sum
        push(x_tx.at[sweep], x_rx.at[sweep], base + 1, x_peers)
        if sweep == 0:
            student_peak = logits(sf_ref, soft, False)
        wait_all(x_rx.at[sweep], recv.at[base + 1])
        y_sum = x_sum + jnp.sum(x_rx[sweep], axis=0)
        y_tx[sweep] = y_sum
        push(y_tx.at[sweep], y_rx.at[sweep], base + 2, y_peers)
        if sweep == 0:
            acc[...] = jnp.zeros(acc.shape, jnp.float32)
            powers(soft, STUDENT, 0, BLOCKS, True)
            student_total = row_sum()
            s_tx[0:1] = student_peak
            s_tx[1:2] = student_total
            push(s_tx, s_rx, 1, z_peers)
        wait_all(y_rx.at[sweep], recv.at[base + 2])
        p_half = 1.0 / (y_sum + jnp.sum(y_rx[sweep], axis=0))
        p_ref[sweep, mine, :] = p_half
        pltpu.make_async_remote_copy(
            src_ref=p_ref.at[sweep, mine], dst_ref=p_ref.at[sweep, mine],
            send_sem=send.at[base + 3], recv_sem=recv.at[base + 3],
            device_id=partner, device_id_type=MESH,
        ).start()
        wait_all(p_ref.at[sweep, other], recv.at[base + 3])

        acc[...] = jnp.zeros(acc.shape, jnp.float32)

        def row_block(b, c):
            part = acc[...]
            for s in range(TILES):
                part += expo[b, :, s * 128:(s + 1) * 128] * p_ref[sweep, pl.ds(b * TILES + s, 1), :]
            acc[...] = part
            return c

        lax.fori_loop(0, BLOCKS, row_block, 0)
        local_row = row_sum() * factor
        z_tx[1 + sweep] = local_row
        push(z_tx.at[1 + sweep], z_rx.at[1 + sweep], base + 4, z_peers)
        if sweep == SWEEPS - 1:
            wait_all(s_rx, recv.at[1])
            top = jnp.maximum(jnp.max(s_rx[:, 0:1], axis=0), student_peak)
            total = student_total * jnp.exp2((student_peak - top) * STUDENT)
            for k in range(NZ - 1):
                total += s_rx[k, 1:2] * jnp.exp2((s_rx[k, 0:1] - top) * STUDENT)
            g_b[...] = to_rows(live * jnp.exp2((student_peak - top) * STUDENT) / total)
        wait_all(z_rx.at[1 + sweep], recv.at[base + 4])
        row = local_row + jnp.sum(z_rx[1 + sweep], axis=0)
        t_b[...] = to_rows(factor / (row + (1.0 - live)))
        wait_all(core_rx.at[sweep], send.at[base])
        wait_all(x_rx.at[sweep], send.at[base + 1])
        wait_all(y_rx.at[sweep], send.at[base + 2])
        wait_all(p_ref.at[sweep, other], send.at[base + 3])
        wait_all(z_rx.at[1 + sweep], send.at[base + 4])
    wait_all(z_rx.at[0], send.at[0])
    wait_all(s_rx, send.at[1])

    def store(b):
        span = pl.ds(pl.multiple_of(b * WIDE, WIDE), WIDE)
        return (
            pltpu.make_async_copy(tgt.at[b], out_hbm.at[:, span], out_sem.at[0, b]),
            pltpu.make_async_copy(wpart.at[b], weight_hbm.at[:, span], out_sem.at[1, b]),
        )

    feature_ref[...] = jnp.zeros(feature_ref.shape, jnp.float32)

    def final_block(b, c):
        for s in range(WIDE // 256):
            halves = []
            for h in range(2):
                lanes = slice(s * 256 + h * 128, s * 256 + (h + 1) * 128)
                target = expo[b, :, lanes] * t_b[...] * p_ref[
                    SWEEPS - 1, pl.ds(b * TILES + s * 2 + h, 1), :]
                tgt[b, :, lanes] = target.astype(jnp.bfloat16)
                halves.append((soft[b, :, lanes] * g_b[...] - target).astype(jnp.bfloat16))
            delta = jnp.concatenate(halves, axis=1)
            span = slice(s * 256, (s + 1) * 256)
            feature_ref[...] += lax.dot_general(
                delta, w[b, :, span], (((1,), (1,)), ((), ())), preferred_element_type=jnp.float32
            )
            wpart[b, :, span] = jnp.dot(sft[...], delta, preferred_element_type=jnp.float32)
        for copy in store(b):
            copy.start()
        return c

    lax.fori_loop(0, BLOCKS, final_block, 0)

    def drain(b, c):
        for copy in store(b):
            copy.wait()
        return c

    lax.fori_loop(0, BLOCKS, drain, 0)


def fused(tf, sf, mask, w):
    d, protos = w.shape
    f32, bf16 = jnp.float32, jnp.bfloat16
    vec = BLOCKS * TILES
    groups = 2 + 5 * SWEEPS
    table = pltpu.VMEM((BLOCKS, ROWS, WIDE), f32)
    rows = pltpu.VMEM((ROWS, 128), f32)
    return pl.pallas_call(
        kernel,
        out_shape=(
            jax.ShapeDtypeStruct((ROWS, protos), bf16),
            jax.ShapeDtypeStruct((d, protos), f32),
            jax.ShapeDtypeStruct((ROWS, d), f32),
        ),
        in_specs=[pl.BlockSpec(memory_space=pltpu.VMEM)] * 3 + [pl.BlockSpec(memory_space=pl.ANY)],
        out_specs=(
            pl.BlockSpec(memory_space=pl.ANY),
            pl.BlockSpec(memory_space=pl.ANY),
            pl.BlockSpec(memory_space=pltpu.VMEM),
        ),
        scratch_shapes=[
            pltpu.VMEM((BLOCKS, d, WIDE), bf16),
            table, table, rows, rows, rows, rows,
            pltpu.VMEM((d, ROWS), bf16),
            pltpu.VMEM((BLOCKS, ROWS, WIDE), bf16),
            pltpu.VMEM((BLOCKS, d, WIDE), f32),
            pltpu.VMEM((vec, 128), f32),
            pltpu.VMEM((SWEEPS, 1, vec // 2, 128), f32),
            pltpu.VMEM((SWEEPS, vec // 2, 128), f32),
            pltpu.VMEM((SWEEPS, NX - 1, vec // 2, 128), f32),
            pltpu.VMEM((SWEEPS, vec // 2, 128), f32),
            pltpu.VMEM((SWEEPS, NY - 1, vec // 2, 128), f32),
            pltpu.VMEM((SWEEPS, vec, 128), f32),
            pltpu.VMEM((SWEEPS + 1, 1, ROWS), f32),
            pltpu.VMEM((SWEEPS + 1, NZ - 1, 1, ROWS), f32),
            pltpu.VMEM((2, ROWS), f32),
            pltpu.VMEM((NZ - 1, 2, ROWS), f32),
            pltpu.SemaphoreType.DMA((BLOCKS,)),
            pltpu.SemaphoreType.DMA((2, BLOCKS)),
            pltpu.SemaphoreType.DMA((groups,)),
            pltpu.SemaphoreType.DMA((groups,)),
        ],
        compiler_params=pltpu.CompilerParams(
            collective_id=0, has_side_effects=True, vmem_limit_bytes=56 * 2**20
        ),
        name="sinkhorn",
    )(tf, sf, mask, w)


def on_device(teacher_feats, student_feats, proto_weight, token_mask):
    targets, weight_part, feature_part = fused(
        teacher_feats, student_feats, token_mask.reshape(1, -1), proto_weight
    )
    feature_grad = lax.psum_scatter(feature_part, "proto", scatter_dimension=1, tiled=True)
    weight_grad = lax.psum_scatter(weight_part, "dp", scatter_dimension=0, tiled=True)
    return targets, weight_grad, feature_grad


def solution(mesh):
    placed = (P("dp", None), P("dp", None), P(None, "proto"), P("dp"))
    return jax.shard_map(
        on_device,
        mesh=mesh,
        in_specs=placed,
        out_specs=(P("dp", "proto"), P("dp", "proto"), P("dp", "proto")),
        check_vma=False,
    )
```

time: 649 us -> 222 us (0.34)
  blocking collectives: 429 us -> 0 us
  Pallas kernels: 0 us -> 65.8 us
  other arithmetic: 47.2 us -> 0 us
  matrix products: 20.3 us -> 0 us
  waiting for transfers between devices: 126 us -> 135 us
    psum x6 -> x0, blocking collectives: 412 us -> none  [the longest x3 378 us: on_device(): column_total = lax.psum(jnp.sum(target, axis=0), 'dp')]
    reduce_scatter x1, waiting for transfers between devices: 18.2 us -> 107 us  [on_device(): lax.psum_scatter(weight_part, 'dp', scatter_dimension=0, tiled=True)]
    unnamed x3, waiting for transfers between devices: 108 us -> 27.6 us
    pallas_call x0 -> x1, Pallas kernels: none -> 65.8 us  [fused(): pl.pallas_call(kernel, out_shape=(jax.ShapeDtypeStruct((ROWS, protos), bf...]
    reduce_sum x7 -> x0, other arithmetic: 35.7 us -> none  [the longest x3 16 us: on_device(): column_total = lax.psum(jnp.sum(target, axis=0), 'dp')]
    dot_general x4 -> x0, matrix products: 20.3 us -> none  [the longest x1 7.01 us: on_device(): jnp.dot(teacher_feats, proto_weight, preferred_element_type=jnp.float32)]
    pmax x1 -> x0, blocking collectives: 17.3 us -> none  [on_device(): row_peak = lax.pmax(jnp.max(teacher_logits, axis=1), 'proto')]
    convert_element_type x2 -> x0, other arithmetic: 11.4 us -> none  [the longest x1 10.6 us: on_device(): (live_rows[:, None] * (jnp.exp(student_logits - lse_rows[:, None]) - targ...]
  transfers between devices with their start and end apart: 2 -> 2, of which waited for: 2 -> 2; matrix products, arithmetic and copies ran while one was open for 2% -> 0% of each run, Pallas kernels for 0% -> 0%
where the time goes in v1:
time: 222 us; the launch traced here: 221 us
  waiting for transfers between devices  135 us (61%)
  Pallas kernels  65.8 us (30%)
  between operations  14 us (6%)
  local copies, waits for them, and re-layouts  6.42 us (3%)
    reduce_scatter x1, waiting for transfers between devices, on_device(): lax.psum_scatter(weight_part, 'dp', scatter_dimension=0, tiled=True)  107 us
    pallas_call x1, Pallas kernels, fused(): pl.pallas_call(kernel, out_shape=(jax.ShapeDtypeStruct((ROWS, protos), bf...  65.8 us
    unnamed x3, waiting for transfers between devices  27.6 us
    unnamed x2, local copies, waits for them, and re-layouts  6.42 us
  transfers between devices with their start and end apart: 2, of which 2 were waited for; matrix products, arithmetic and copies ran while one was open for 0% of the time, Pallas kernels for 0%

profile of v1, /device:TPU:1, one launch (start us, length us, event | category | flops | bytes accessed | tf_op | source)
XLA Modules:
  0.0 221.3 jit_solution(12611984610052888447)
XLA Ops:
  7.2 0.0 reduce-scatter.7.cloned.1.call-start
  7.2 65.8 %sinkhorn.1 = (bf16[256,8192]{1,0:T(8,128)(2,1)}, f32[256,8192]{1,0:T(8,128)}, f32[256,256]{1,0:T(8,128)}) custom-call(bf16[256,256]{1,0:T(8,128)(2,1)} %tf_ref.1, bf16[256,256]{1,0:T(8,128)(2,1)} %sf_ref.1, s32[1,256]{1,0:T(1,128)} %bitcast.4, bf16[256,8192]{1,0:T(8,128)(2,1)} %w_hbm.1), custom_call_target="tpu_custom_call" | custom-call | tf_op jit(solution)/shard_map/sinkhorn/pallas_call | solution.py:236
  73.1 1.8 copy.9
  74.8 0.0 reduce-scatter.7.cloned.1.call-update
  74.9 0.0 reduce-scatter.5.cloned.1.call-start
  74.9 0.7 reduce-scatter.5.cloned.1.call-update
  75.6 26.8 %reduce-scatter.7.cloned.1.call-done = f32[32,256]{1,0:T(8,128)} async-done(((f32[256,256]{1,0:T(8,128)}), f32[32,256]{1,0:T(8,128)}) %reduce-scatter.7.cloned.1.call-update) | async-done | bytes 32784
  102.5 107.4 %reduce-scatter.5.cloned.1.call-done = f32[8,8192]{1,0:T(8,128)} async-done(((f32[256,8192]{1,0:T(8,128)}), f32[8,8192]{1,0:T(8,128)}) %reduce-scatter.5.cloned.1.call-update) | async-done | bytes 262160 | tf_op jit(solution)/shard_map/reduce_scatter | solution.py:283
  209.8 4.6 %copy.12 = bf16[256,8192]{1,0:T(8,128)(2,1)} copy(bf16[256,8192]{1,0:T(8,128)(2,1)} %get-tuple-element.18) | data formatting | bytes 8388608
Async XLA Ops:
  7.2 95.3 %reduce-scatter.7.cloned.1.call-start = ((), (), s32[]{:S(2)}) async-start(), calls=%async_computation.3 | async-start | bytes 294912
  74.9 135.0 %reduce-scatter.5.cloned.1.call-start = ((), (), s32[]{:S(2)}) async-start(), calls=%async_computation.2 | async-start | bytes 8650752 | tf_op jit(solution)/shard_map/reduce_scatter | solution.py:283
Sparse Core Ops, SparseCore 0:
  75.0 27.4 reduce-scatter.6
  107.6 102.2 reduce-scatter.4

commit v2 on v1

v2 whole, which is shorter than its diff:
```python
import math

import jax
import jax.numpy as jnp
from jax import lax
from jax.experimental import pallas as pl
from jax.experimental.pallas import tpu as pltpu
from jax.sharding import PartitionSpec as P

SWEEPS = 3
TEACHER = math.log2(math.e) / 0.07
STUDENT = math.log2(math.e) / 0.1
MESH = pl.DeviceIdType.MESH
NX, NY, NC, NZ = 4, 4, 2, 8
ROWS = 256
WIDE = 1024
BLOCKS = 8
TILES = WIDE // 128
PARTS = WIDE // 256
NT = (((1,), (1,)), ((), ()))
BASE = 8
PEAK, TOTALS, FEATS, RELAY, SCALARS, TOKENS, FEATURE, SPREAD = range(BASE)
RS = BASE + 5 * SWEEPS


def wait_all(ref, sem):
    pltpu.make_async_copy(ref, ref, sem).wait()


def to_rows(lanes, width=ROWS):
    return jnp.transpose(jnp.broadcast_to(lanes, (128, width)))


def kernel(
    tf_ref, sf_ref, mask_ref, w_hbm,
    out_hbm, weight_ref, feature_ref,
    w, expo, soft, peak_b, acc, t_b, g_b, tgt, delta_a, fpt, f_rx,
    wt, eb, qb, gall, sft, dcat, pcol, scal, tall, wp_tx, rs_rx, a_tx, a_rx,
    col_tx, core_rx, x_tx, x_rx, y_tx, y_rx, p_ref,
    z_tx, z_rx, s_tx, s_rx,
    w_sem, out_sem, send, recv,
):
    dp = lax.axis_index("dp")
    z = lax.axis_index("proto")
    cx, cy, cc = dp // (NY * NC), lax.rem(dp // NC, NY), lax.rem(dp, NC)

    def at(x, y, c):
        return {"dp": (x * NY + y) * NC + c}

    def row_place(n):
        x = lax.rem(cx + n % NX, NX)
        return x, (cc if n < NX else 1 - cc)

    def row_source(n):
        x = lax.rem(cx + NX - n % NX, NX)
        return x * NC + (cc if n < NX else 1 - cc)

    partner = at(cx, cy, 1 - cc)
    row_peers = [at(row_place(n)[0], cy, row_place(n)[1]) for n in range(1, BLOCKS)]
    x_peers = row_peers[: NX - 1]
    y_peers = [at(cx, lax.rem(cy + k, NY), cc) for k in range(1, NY)]
    z_place = [lax.rem(z + k, NZ) for k in range(1, NZ)]
    z_peers = [{"proto": place} for place in z_place]
    mine_g = cx * NC + cc

    barrier = pltpu.get_barrier_semaphore()
    peers = row_peers + y_peers + z_peers
    for peer in peers:
        pl.semaphore_signal(barrier, inc=1, device_id=peer, device_id_type=MESH)

    def load(b):
        return pltpu.make_async_copy(
            w_hbm.at[:, pl.ds(pl.multiple_of(b * WIDE, WIDE), WIDE)], w.at[b], w_sem.at[b]
        )

    def start_load(b, c):
        load(b).start()
        return c

    lax.fori_loop(0, BLOCKS, start_load, 0)

    def send_one(src, dst, group, device):
        pltpu.make_async_remote_copy(
            src_ref=src, dst_ref=dst, send_sem=send.at[group], recv_sem=recv.at[group],
            device_id=device, device_id_type=MESH,
        ).start()

    def push(src, dst, group, devices):
        for k, device in enumerate(devices):
            send_one(src, dst.at[k], group, device)

    def logits(feats_ref, table, first):
        acc[...] = jnp.full(acc.shape, -jnp.inf, jnp.float32)

        def block(b, c):
            if first:
                load(b).wait()
            for s in range(PARTS):
                part = jnp.dot(
                    feats_ref[...], w[b, :, s * 256:(s + 1) * 256],
                    preferred_element_type=jnp.float32,
                )
                table[b, :, s * 256:(s + 1) * 256] = part
                acc[...] = jnp.maximum(acc[...], jnp.maximum(part[:, :128], part[:, 128:]))
            return c

        lax.fori_loop(0, BLOCKS, block, 0)
        peak_b[...] = jnp.broadcast_to(jnp.max(acc[...], axis=1, keepdims=True), acc.shape)
        return jnp.max(jnp.transpose(acc[...]), axis=0, keepdims=True)

    def powers(table, scale, total):
        def block(b, c):
            for s in range(TILES):
                at_s = (b, slice(None), slice(s * 128, (s + 1) * 128))
                value = jnp.exp2((table[at_s] - peak_b[...]) * scale)
                table[at_s] = value
                if total:
                    acc[...] += value
            return c

        lax.fori_loop(0, BLOCKS, block, 0)

    def row_sum():
        return jnp.sum(jnp.transpose(acc[...]), axis=0, keepdims=True)

    def shared_tables(n, c):
        feats_t = gall[n, 0].astype(jnp.bfloat16)
        feats_s = gall[n, 1].astype(jnp.bfloat16)
        sft[:, pl.ds(pl.multiple_of(n * ROWS, ROWS), ROWS)] = feats_s
        for q in range(PARTS):
            rows = slice(q * 256, (q + 1) * 256)
            dot = jnp.dot(wt[rows, :], feats_t, preferred_element_type=jnp.float32)
            eb[n, rows, :] = jnp.exp2((dot - scal[n, 0:1]) * TEACHER)
            dot = jnp.dot(wt[rows, :], feats_s, preferred_element_type=jnp.float32)
            qb[n, rows, :] = jnp.exp2((dot - scal[n, 1:2]) * STUDENT) * scal[n, 2:3]
        return c

    live = mask_ref[...].astype(jnp.float32)

    local_peak = logits(tf_ref, expo, True)
    z_tx[0] = local_peak
    gall[0, 0] = jnp.transpose(tf_ref[...].astype(jnp.float32))
    gall[0, 1] = jnp.transpose(sf_ref[...].astype(jnp.float32))
    pl.semaphore_wait(barrier, len(peers))
    push(z_tx.at[0], z_rx.at[0], PEAK, z_peers)
    for n in range(1, NX):
        send_one(gall.at[0], gall.at[n], FEATS, x_peers[n - 1])
    send_one(gall.at[0], gall.at[NX], RELAY, partner)
    powers(expo, TEACHER, False)
    wait_all(z_rx.at[0], recv.at[PEAK])
    joint_peak = jnp.maximum(jnp.max(z_rx[0], axis=0), local_peak)
    factor = live * jnp.exp2((local_peak - joint_peak) * TEACHER)
    t_b[...] = to_rows(factor)

    for sweep in range(SWEEPS):
        base = BASE + 5 * sweep

        def column_block(b, c):
            for s in range(TILES):
                col = expo[b, :, s * 128:(s + 1) * 128] * t_b[...]
                col_tx[pl.ds(b * TILES + s, 1), :] = jnp.sum(col, axis=0, keepdims=True)
            return c

        lax.fori_loop(0, BLOCKS, column_block, 0)
        half = BLOCKS * TILES // 2
        mine = pl.ds(pl.multiple_of(cc * half, half), half)
        other = pl.ds(pl.multiple_of((1 - cc) * half, half), half)
        push(col_tx.at[other], core_rx.at[sweep], base, [partner])
        wait_all(core_rx.at[sweep], recv.at[base])
        x_sum = col_tx[mine, :] + core_rx[sweep, 0]
        x_tx[sweep] = x_sum
        push(x_tx.at[sweep], x_rx.at[sweep], base + 1, x_peers)
        if sweep == 0:
            student_peak = logits(sf_ref, soft, False)
        if sweep == 1:
            wait_all(gall.at[pl.ds(1, NX - 1)], recv.at[FEATS])
            for n in range(1, NX):
                send_one(gall.at[n], gall.at[NX + n], RELAY, partner)
        if sweep == 2:
            lax.fori_loop(NX, BLOCKS, shared_tables, 0)
        wait_all(x_rx.at[sweep], recv.at[base + 1])
        y_sum = x_sum + jnp.sum(x_rx[sweep], axis=0)
        y_tx[sweep] = y_sum
        push(y_tx.at[sweep], y_rx.at[sweep], base + 2, y_peers)
        if sweep == 0:
            acc[...] = jnp.zeros(acc.shape, jnp.float32)
            powers(soft, STUDENT, True)
            student_total = row_sum()
            s_tx[0:1] = student_peak
            s_tx[1:2] = student_total
            push(s_tx, s_rx, TOTALS, z_peers)
        if sweep == 1:
            wait_all(scal.at[pl.ds(1, BLOCKS - 1)], recv.at[SCALARS])
            lax.fori_loop(0, 2, shared_tables, 0)
        wait_all(y_rx.at[sweep], recv.at[base + 2])
        p_half = 1.0 / (y_sum + jnp.sum(y_rx[sweep], axis=0))
        p_ref[sweep, mine, :] = p_half
        send_one(p_ref.at[sweep, mine], p_ref.at[sweep, mine], base + 3, partner)
        wait_all(p_ref.at[sweep, other], recv.at[base + 3])

        acc[...] = jnp.zeros(acc.shape, jnp.float32)

        def row_block(b, c):
            part = acc[...]
            for s in range(TILES):
                part += expo[b, :, s * 128:(s + 1) * 128] * p_ref[sweep, pl.ds(b * TILES + s, 1), :]
            acc[...] = part
            return c

        lax.fori_loop(0, BLOCKS, row_block, 0)
        local_row = row_sum() * factor
        z_tx[1 + sweep] = local_row
        push(z_tx.at[1 + sweep], z_rx.at[1 + sweep], base + 4, z_peers)
        if sweep == 0:
            wt[...] = jnp.transpose(w[mine_g])
            wait_all(s_rx, recv.at[TOTALS])
            top = jnp.maximum(jnp.max(s_rx[:, 0:1], axis=0), student_peak)
            total = student_total * jnp.exp2((student_peak - top) * STUDENT)
            for k in range(NZ - 1):
                total += s_rx[k, 1:2] * jnp.exp2((s_rx[k, 0:1] - top) * STUDENT)
            share = live * jnp.exp2((student_peak - top) * STUDENT) / total
            g_b[...] = to_rows(share)
            scal[0, 0:1] = local_peak
            scal[0, 1:2] = student_peak
            scal[0, 2:3] = share
            for n in range(1, BLOCKS):
                send_one(scal.at[0], scal.at[n], SCALARS, row_peers[n - 1])
        if sweep == 1:
            lax.fori_loop(2, NX, shared_tables, 0)
            wait_all(gall.at[pl.ds(NX, NX)], recv.at[RELAY])
        if sweep == SWEEPS - 1:
            for s in range(TILES):
                pcol[s * 128:(s + 1) * 128, :] = to_rows(
                    p_ref[sweep, pl.ds(mine_g * TILES + s, 1), :], 128)
        wait_all(z_rx.at[1 + sweep], recv.at[base + 4])
        row = local_row + jnp.sum(z_rx[1 + sweep], axis=0)
        scale = factor / (row + (1.0 - live))
        if sweep == SWEEPS - 1:
            tall[0] = scale
            for n in range(1, BLOCKS):
                send_one(tall.at[0], tall.at[n], TOKENS, row_peers[n - 1])
        t_b[...] = to_rows(scale)
        wait_all(core_rx.at[sweep], send.at[base])
        wait_all(x_rx.at[sweep], send.at[base + 1])
        wait_all(y_rx.at[sweep], send.at[base + 2])
        wait_all(p_ref.at[sweep, other], send.at[base + 3])
        wait_all(z_rx.at[1 + sweep], send.at[base + 4])

    def store(b):
        span = pl.ds(pl.multiple_of(b * WIDE, WIDE), WIDE)
        return pltpu.make_async_copy(tgt.at[b], out_hbm.at[:, span], out_sem.at[b])

    fpt[...] = jnp.zeros(fpt.shape, jnp.float32)

    def own_block(b, c):
        for s in range(TILES):
            lanes = slice(s * 128, (s + 1) * 128)
            target = expo[b, :, lanes] * t_b[...] * p_ref[SWEEPS - 1, pl.ds(b * TILES + s, 1), :]
            tgt[b, :, lanes] = target.astype(jnp.bfloat16)
            delta_a[:, lanes] = (soft[b, :, lanes] * g_b[...] - target).astype(jnp.bfloat16)
        fpt[...] += lax.dot_general(
            w[b], delta_a[...], NT, preferred_element_type=jnp.float32
        ).reshape(fpt.shape)
        store(b).start()
        return c

    def shared_part(q, c):
        rows = pl.ds(pl.multiple_of(q * 256, 256), 256)
        for n in range(BLOCKS):
            for h in range(2):
                lanes = slice(h * 128, (h + 1) * 128)
                target = eb[n, rows, lanes] * pcol[rows, :] * tall[n, :, lanes]
                dcat[:, n * ROWS + h * 128:n * ROWS + (h + 1) * 128] = (
                    qb[n, rows, lanes] - target).astype(jnp.bfloat16)
        grad = lax.dot_general(sft[...], dcat[...], NT, preferred_element_type=jnp.float32)
        for x in range(NX):
            for y in range(NY):
                top = (x * NY + y) * 16
                wp_tx[q, y, x * 16:(x + 1) * 16, :] = grad[top:top + 16]
        for k in range(1, NY):
            send_one(wp_tx.at[q, lax.rem(cy + k, NY)], rs_rx.at[q, k - 1], RS + q, y_peers[k - 1])
        return c

    lax.fori_loop(0, BLOCKS // 2, own_block, 0)
    wait_all(tall.at[pl.ds(1, BLOCKS - 1)], recv.at[TOKENS])
    lax.fori_loop(0, PARTS, shared_part, 0)
    lax.fori_loop(BLOCKS // 2, BLOCKS, own_block, 0)
    for k in range(1, NZ):
        send_one(fpt.at[z_place[k - 1]], f_rx.at[k - 1], FEATURE, z_peers[k - 1])

    def collect(q, c):
        wait_all(rs_rx.at[q], recv.at[RS + q])
        grad = wp_tx[q, cy] + jnp.sum(rs_rx[q], axis=0)
        a_tx[q] = grad.reshape(BLOCKS, 8, 256)
        for n in range(1, BLOCKS):
            x, core = row_place(n)
            send_one(a_tx.at[q, x * NC + core], a_rx.at[q, n - 1], SPREAD, row_peers[n - 1])
        return c

    lax.fori_loop(0, PARTS, collect, 0)
    wait_all(f_rx, recv.at[FEATURE])
    feature_ref[...] = jnp.transpose(fpt[z] + jnp.sum(f_rx[...], axis=0))
    wait_all(a_rx, recv.at[SPREAD])
    for q in range(PARTS):
        for n in range(BLOCKS):
            span = pl.ds(pl.multiple_of(row_source(n) * WIDE + q * 256, 256), 256)
            weight_ref[:, span] = a_rx[q, n - 1] if n else a_tx[q, mine_g]

    def drain(b, c):
        store(b).wait()
        return c

    lax.fori_loop(0, BLOCKS, drain, 0)
    wait_all(z_rx.at[0], send.at[PEAK])
    wait_all(s_rx, send.at[TOTALS])
    wait_all(gall.at[pl.ds(1, NX - 1)], send.at[FEATS])
    wait_all(gall.at[pl.ds(NX, NX)], send.at[RELAY])
    wait_all(scal.at[pl.ds(1, BLOCKS - 1)], send.at[SCALARS])
    wait_all(tall.at[pl.ds(1, BLOCKS - 1)], send.at[TOKENS])
    wait_all(f_rx, send.at[FEATURE])
    wait_all(a_rx, send.at[SPREAD])
    for q in range(PARTS):
        wait_all(rs_rx.at[q], send.at[RS + q])


def on_device(teacher_feats, student_feats, proto_weight, token_mask):
    d, protos = proto_weight.shape
    f32, bf16 = jnp.float32, jnp.bfloat16
    vec = BLOCKS * TILES
    groups = RS + PARTS
    table = pltpu.VMEM((BLOCKS, ROWS, WIDE), f32)
    shared = pltpu.VMEM((BLOCKS, WIDE, ROWS), f32)
    rows = pltpu.VMEM((ROWS, 128), f32)
    vmem = pl.BlockSpec(memory_space=pltpu.VMEM)
    hbm = pl.BlockSpec(memory_space=pl.ANY)
    return pl.pallas_call(
        kernel,
        out_shape=(
            jax.ShapeDtypeStruct((ROWS, protos), bf16),
            jax.ShapeDtypeStruct((d // (NX * NY * NC), protos), f32),
            jax.ShapeDtypeStruct((ROWS, d // NZ), f32),
        ),
        in_specs=[vmem, vmem, vmem, hbm],
        out_specs=(hbm, vmem, vmem),
        scratch_shapes=[
            pltpu.VMEM((BLOCKS, d, WIDE), bf16),
            table, table, rows, rows, rows, rows,
            pltpu.VMEM((BLOCKS, ROWS, WIDE), bf16),
            pltpu.VMEM((ROWS, WIDE), bf16),
            pltpu.VMEM((NZ, d // NZ, ROWS), f32),
            pltpu.VMEM((NZ - 1, d // NZ, ROWS), f32),
            pltpu.VMEM((WIDE, d), bf16),
            shared, shared,
            pltpu.VMEM((BLOCKS, 2, d, ROWS), f32),
            pltpu.VMEM((d, BLOCKS * ROWS), bf16),
            pltpu.VMEM((256, BLOCKS * ROWS), bf16),
            pltpu.VMEM((WIDE, 128), f32),
            pltpu.VMEM((BLOCKS, 3, ROWS), f32),
            pltpu.VMEM((BLOCKS, 1, ROWS), f32),
            pltpu.VMEM((PARTS, NY, d // NY, 256), f32),
            pltpu.VMEM((PARTS, NY - 1, d // NY, 256), f32),
            pltpu.VMEM((PARTS, BLOCKS, 8, 256), f32),
            pltpu.VMEM((PARTS, BLOCKS - 1, 8, 256), f32),
            pltpu.VMEM((vec, 128), f32),
            pltpu.VMEM((SWEEPS, 1, vec // 2, 128), f32),
            pltpu.VMEM((SWEEPS, vec // 2, 128), f32),
            pltpu.VMEM((SWEEPS, NX - 1, vec // 2, 128), f32),
            pltpu.VMEM((SWEEPS, vec // 2, 128), f32),
            pltpu.VMEM((SWEEPS, NY - 1, vec // 2, 128), f32),
            pltpu.VMEM((SWEEPS, vec, 128), f32),
            pltpu.VMEM((SWEEPS + 1, 1, ROWS), f32),
            pltpu.VMEM((SWEEPS + 1, NZ - 1, 1, ROWS), f32),
            pltpu.VMEM((2, ROWS), f32),
            pltpu.VMEM((NZ - 1, 2, ROWS), f32),
            pltpu.SemaphoreType.DMA((BLOCKS,)),
            pltpu.SemaphoreType.DMA((BLOCKS,)),
            pltpu.SemaphoreType.DMA((groups,)),
            pltpu.SemaphoreType.DMA((groups,)),
        ],
        compiler_params=pltpu.CompilerParams(
            collective_id=0, has_side_effects=True, vmem_limit_bytes=60 * 2**20
        ),
        name="sinkhorn",
    )(teacher_feats, student_feats, token_mask.reshape(1, -1), proto_weight)


def solution(mesh):
    placed = (P("dp", None), P("dp", None), P(None, "proto"), P("dp"))
    return jax.shard_map(
        on_device,
        mesh=mesh,
        in_specs=placed,
        out_specs=(P("dp", "proto"), P("dp", "proto"), P("dp", "proto")),
        check_vma=False,
    )
```

time: 222 us -> 107 us (0.48)
  waiting for transfers between devices: 135 us -> 0 us
  Pallas kernels: 65.8 us -> 99.2 us
  between operations: 14 us -> 0.64 us
    reduce_scatter x1 -> x0, waiting for transfers between devices: 107 us -> none  [on_device(): lax.psum_scatter(weight_part, 'dp', scatter_dimension=0, tiled=True)]
    pallas_call x1, Pallas kernels: 65.8 us -> 99.2 us  [on_device(): pl.pallas_call(kernel, out_shape=(jax.ShapeDtypeStruct((ROWS, protos), bf...]
    unnamed x3 -> x0, waiting for transfers between devices: 27.6 us -> none
    unnamed x2 -> x4, local copies, waits for them, and re-layouts: 6.42 us -> 5.39 us
  transfers between devices with their start and end apart: 2 -> 0, of which waited for: 2 -> 0; matrix products, arithmetic and copies ran while one was open for 0% -> 0% of each run, Pallas kernels for 0% -> 0%
where the time goes in v2:
time: 107 us
  Pallas kernels  99.2 us (93%)
  local copies, waits for them, and re-layouts  6.98 us (7%)
    pallas_call x1, Pallas kernels, on_device(): pl.pallas_call(kernel, out_shape=(jax.ShapeDtypeStruct((ROWS, protos), bf...  99.2 us
    unnamed x4, local copies, waits for them, and re-layouts  5.39 us

profile of v2, /device:TPU:1, one launch (start us, length us, event | category | flops | bytes accessed | tf_op | source)
XLA Modules:
  0.0 106.8 jit_solution(12788422859394921382)
XLA Ops:
  0.6 99.2 %sinkhorn.1 = (bf16[256,8192]{1,0:T(8,128)(2,1)}, f32[8,8192]{1,0:T(8,128)}, f32[256,32]{1,0:T(8,128)}) custom-call(bf16[256,256]{1,0:T(8,128)(2,1)} %tf_ref.1, bf16[256,256]{1,0:T(8,128)(2,1)} %sf_ref.1, s32[1,256]{1,0:T(1,128)} %bitcast.1, bf16[256,8192]{1,0:T(8,128)(2,1)} %w_hbm.1), custom_call_target="tpu_custom_call" | custom-call | tf_op jit(solution)/shard_map/sinkhorn/pallas_call | solution.py:336
  99.8 1.6 %copy.7 = f32[256,32]{0,1:T(8,128)} copy(f32[256,32]{1,0:T(8,128)} %get-tuple-element.5) | data formatting | bytes 65536 | tf_op jit(solution)/shard_map/sinkhorn/pallas_call | solution.py:336
  101.4 0.0 copy-start
  101.4 4.7 %copy.10 = bf16[256,8192]{1,0:T(8,128)(2,1)} copy(bf16[256,8192]{1,0:T(8,128)(2,1)} %get-tuple-element.9) | data formatting | bytes 8388608
  106.1 0.0 copy-done
  106.1 0.7 copy.11
Async XLA Ops:
  101.4 4.7 %copy-start = (f32[8,8192]{1,0:T(8,128)S(1)}, f32[8,8192]{1,0:T(8,128)}, u32[]{:S(2)}) copy-start(f32[8,8192]{1,0:T(8,128)} %get-tuple-element.10) | copy-start | bytes 786436

commit v3 on v2

--- a/solution.py
+++ b/solution.py
@@ -33,12 +33,12 @@
 
 def kernel(
     tf_ref, sf_ref, mask_ref, w_hbm,
-    out_hbm, weight_ref, feature_ref,
-    w, expo, soft, peak_b, acc, t_b, g_b, tgt, delta_a, fpt, f_rx,
+    tgt, weight_ref, feature_ref,
+    w, expo, soft, peak_b, acc, t_b, g_b, delta_a, fpt, f_rx,
     wt, eb, qb, gall, sft, dcat, pcol, scal, tall, wp_tx, rs_rx, a_tx, a_rx,
     col_tx, core_rx, x_tx, x_rx, y_tx, y_rx, p_ref,
     z_tx, z_rx, s_tx, s_rx,
-    w_sem, out_sem, send, recv,
+    w_sem, send, recv,
 ):
     dp = lax.axis_index("dp")
     z = lax.axis_index("proto")
@@ -88,6 +88,15 @@
     def push(src, dst, group, devices):
         for k, device in enumerate(devices):
             send_one(src, dst.at[k], group, device)
+
+    def gather(first, last):
+        def piece(q, c):
+            for n in range(1, NX):
+                at_q = (q // 4, pl.ds(pl.multiple_of(q % 4 * 64, 64), 64))
+                send_one(gall.at[(0,) + at_q], gall.at[(n,) + at_q], FEATS, x_peers[n - 1])
+            return c
+
+        lax.fori_loop(first, last, piece, 0)
 
     def logits(feats_ref, table, first):
         acc[...] = jnp.full(acc.shape, -jnp.inf, jnp.float32)
@@ -143,8 +152,7 @@
     gall[0, 1] = jnp.transpose(sf_ref[...].astype(jnp.float32))
     pl.semaphore_wait(barrier, len(peers))
     push(z_tx.at[0], z_rx.at[0], PEAK, z_peers)
-    for n in range(1, NX):
-        send_one(gall.at[0], gall.at[n], FEATS, x_peers[n - 1])
+    gather(0, 2)
     send_one(gall.at[0], gall.at[NX], RELAY, partner)
     powers(expo, TEACHER, False)
     wait_all(z_rx.at[0], recv.at[PEAK])
@@ -172,16 +180,16 @@
         push(x_tx.at[sweep], x_rx.at[sweep], base + 1, x_peers)
         if sweep == 0:
             student_peak = logits(sf_ref, soft, False)
-        if sweep == 1:
-            wait_all(gall.at[pl.ds(1, NX - 1)], recv.at[FEATS])
-            for n in range(1, NX):
-                send_one(gall.at[n], gall.at[NX + n], RELAY, partner)
         if sweep == 2:
-            lax.fori_loop(NX, BLOCKS, shared_tables, 0)
+            lax.fori_loop(0, NX, shared_tables, 0)
         wait_all(x_rx.at[sweep], recv.at[base + 1])
         y_sum = x_sum + jnp.sum(x_rx[sweep], axis=0)
         y_tx[sweep] = y_sum
         push(y_tx.at[sweep], y_rx.at[sweep], base + 2, y_peers)
+        if sweep == 0:
+            gather(2, 6)
+        if sweep == 1:
+            gather(6, 8)
         if sweep == 0:
             acc[...] = jnp.zeros(acc.shape, jnp.float32)
             powers(soft, STUDENT, True)
@@ -189,9 +197,9 @@
             s_tx[0:1] = student_peak
             s_tx[1:2] = student_total
             push(s_tx, s_rx, TOTALS, z_peers)
-        if sweep == 1:
-            wait_all(scal.at[pl.ds(1, BLOCKS - 1)], recv.at[SCALARS])
-            lax.fori_loop(0, 2, shared_tables, 0)
+        if sweep == 2:
+            wait_all(gall.at[pl.ds(NX, NX)], recv.at[RELAY])
+            lax.fori_loop(NX, NX + 3, shared_tables, 0)
         wait_all(y_rx.at[sweep], recv.at[base + 2])
         p_half = 1.0 / (y_sum + jnp.sum(y_rx[sweep], axis=0))
         p_ref[sweep, mine, :] = p_half
@@ -226,9 +234,12 @@
             for n in range(1, BLOCKS):
                 send_one(scal.at[0], scal.at[n], SCALARS, row_peers[n - 1])
         if sweep == 1:
-            lax.fori_loop(2, NX, shared_tables, 0)
-            wait_all(gall.at[pl.ds(NX, NX)], recv.at[RELAY])
+            wait_all(scal.at[pl.ds(1, BLOCKS - 1)], recv.at[SCALARS])
+            wait_all(gall.at[pl.ds(1, NX - 1)], recv.at[FEATS])
+            for n in range(1, NX):
+                send_one(gall.at[n], gall.at[NX + n], RELAY, partner)
         if sweep == SWEEPS - 1:
+            lax.fori_loop(NX + 3, BLOCKS, shared_tables, 0)
             for s in range(TILES):
                 pcol[s * 128:(s + 1) * 128, :] = to_rows(
                     p_ref[sweep, pl.ds(mine_g * TILES + s, 1), :], 128)
@@ -246,22 +257,17 @@
         wait_all(p_ref.at[sweep, other], send.at[base + 3])
         wait_all(z_rx.at[1 + sweep], send.at[base + 4])
 
-    def store(b):
-        span = pl.ds(pl.multiple_of(b * WIDE, WIDE), WIDE)
-        return pltpu.make_async_copy(tgt.at[b], out_hbm.at[:, span], out_sem.at[b])
-
     fpt[...] = jnp.zeros(fpt.shape, jnp.float32)
 
     def own_block(b, c):
         for s in range(TILES):
             lanes = slice(s * 128, (s + 1) * 128)
             target = expo[b, :, lanes] * t_b[...] * p_ref[SWEEPS - 1, pl.ds(b * TILES + s, 1), :]
-            tgt[b, :, lanes] = target.astype(jnp.bfloat16)
+            tgt[:, pl.ds(pl.multiple_of(b * WIDE + s * 128, 128), 128)] = target.astype(jnp.bfloat16)
             delta_a[:, lanes] = (soft[b, :, lanes] * g_b[...] - target).astype(jnp.bfloat16)
         fpt[...] += lax.dot_general(
             w[b], delta_a[...], NT, preferred_element_type=jnp.float32
         ).reshape(fpt.shape)
-        store(b).start()
         return c
 
     def shared_part(q, c):
@@ -299,18 +305,13 @@
 
     lax.fori_loop(0, PARTS, collect, 0)
     wait_all(f_rx, recv.at[FEATURE])
-    feature_ref[...] = jnp.transpose(fpt[z] + jnp.sum(f_rx[...], axis=0))
+    feature_ref[...] = fpt[z] + jnp.sum(f_rx[...], axis=0)
     wait_all(a_rx, recv.at[SPREAD])
     for q in range(PARTS):
         for n in range(BLOCKS):
             span = pl.ds(pl.multiple_of(row_source(n) * WIDE + q * 256, 256), 256)
             weight_ref[:, span] = a_rx[q, n - 1] if n else a_tx[q, mine_g]
 
-    def drain(b, c):
-        store(b).wait()
-        return c
-
-    lax.fori_loop(0, BLOCKS, drain, 0)
     wait_all(z_rx.at[0], send.at[PEAK])
     wait_all(s_rx, send.at[TOTALS])
     wait_all(gall.at[pl.ds(1, NX - 1)], send.at[FEATS])
@@ -323,6 +324,15 @@
         wait_all(rs_rx.at[q], send.at[RS + q])
 
 
+def write_out(*refs):
+    sems = refs[6]
+    copies = [pltpu.make_async_copy(refs[i], refs[3 + i], sems.at[i]) for i in range(3)]
+    for copy in copies:
+        copy.start()
+    for copy in copies:
+        copy.wait()
+
+
 def on_device(teacher_feats, student_feats, proto_weight, token_mask):
     d, protos = proto_weight.shape
     f32, bf16 = jnp.float32, jnp.bfloat16
@@ -333,19 +343,18 @@
     rows = pltpu.VMEM((ROWS, 128), f32)
     vmem = pl.BlockSpec(memory_space=pltpu.VMEM)
     hbm = pl.BlockSpec(memory_space=pl.ANY)
-    return pl.pallas_call(
+    results = pl.pallas_call(
         kernel,
         out_shape=(
-            jax.ShapeDtypeStruct((ROWS, protos), bf16),
-            jax.ShapeDtypeStruct((d // (NX * NY * NC), protos), f32),
-            jax.ShapeDtypeStruct((ROWS, d // NZ), f32),
+            pltpu.VMEM((ROWS, protos), bf16),
+            pltpu.VMEM((d // (NX * NY * NC), protos), f32),
+            pltpu.VMEM((d // NZ, ROWS), f32),
         ),
         in_specs=[vmem, vmem, vmem, hbm],
-        out_specs=(hbm, vmem, vmem),
+        out_specs=(vmem, vmem, vmem),
         scratch_shapes=[
             pltpu.VMEM((BLOCKS, d, WIDE), bf16),
             table, table, rows, rows, rows, rows,
-            pltpu.VMEM((BLOCKS, ROWS, WIDE), bf16),
             pltpu.VMEM((ROWS, WIDE), bf16),
             pltpu.VMEM((NZ, d // NZ, ROWS), f32),
             pltpu.VMEM((NZ - 1, d // NZ, ROWS), f32),
@@ -373,15 +382,24 @@
             pltpu.VMEM((2, ROWS), f32),
             pltpu.VMEM((NZ - 1, 2, ROWS), f32),
             pltpu.SemaphoreType.DMA((BLOCKS,)),
-            pltpu.SemaphoreType.DMA((BLOCKS,)),
             pltpu.SemaphoreType.DMA((groups,)),
             pltpu.SemaphoreType.DMA((groups,)),
         ],
         compiler_params=pltpu.CompilerParams(
-            collective_id=0, has_side_effects=True, vmem_limit_bytes=60 * 2**20
+            collective_id=0, has_side_effects=True, vmem_limit_bytes=54 * 2**20
         ),
         name="sinkhorn",
     )(teacher_feats, student_feats, token_mask.reshape(1, -1), proto_weight)
+    targets, weight_grad, feature_grad = pl.pallas_call(
+        write_out,
+        out_shape=tuple(jax.ShapeDtypeStruct(r.shape, r.dtype) for r in results),
+        in_specs=[hbm] * 3,
+        out_specs=(hbm, hbm, hbm),
+        scratch_shapes=[pltpu.SemaphoreType.DMA((3,))],
+        compiler_params=pltpu.CompilerParams(vmem_limit_bytes=2**20),
+        name="write_out",
+    )(*results)
+    return targets, weight_grad, feature_grad.T
 
 
 def solution(mesh):

time: 107 us -> 85.8 us (0.80)
  Pallas kernels: 99.2 us -> 85 us
  local copies, waits for them, and re-layouts: 6.98 us -> 0 us
    pallas_call x1 -> x2, Pallas kernels: 99.2 us -> 85 us  [the longest x1 82.9 us: on_device(): pl.pallas_call(kernel, out_shape=(pltpu.VMEM((ROWS, protos), bf16), pltpu...]
    unnamed x4 -> x0, local copies, waits for them, and re-layouts: 5.39 us -> none
    pallas_call x1 -> x0, local copies, waits for them, and re-layouts: 1.59 us -> none  [on_device(): pl.pallas_call(kernel, out_shape=(jax.ShapeDtypeStruct((ROWS, protos), bf...]
where the time goes in v3:
time: 85.8 us; the launch traced here: 85.7 us
  Pallas kernels  85 us (99%)
    pallas_call x1, Pallas kernels, on_device(): pl.pallas_call(kernel, out_shape=(pltpu.VMEM((ROWS, protos), bf16), pltpu...  82.9 us
    pallas_call x1, Pallas kernels, on_device(): pl.pallas_call(write_out, out_shape=tuple((jax.ShapeDtypeStruct(r.shape,...  2.11 us

profile of v3, /device:TPU:1, one launch (start us, length us, event | category | flops | bytes accessed | tf_op | source)
XLA Modules:
  0.0 85.7 jit_solution(2840609293770231916)
XLA Ops:
  0.6 82.9 %sinkhorn.1 = (bf16[256,8192]{1,0:T(8,128)(2,1)S(1)}, f32[8,8192]{1,0:T(8,128)S(1)}, f32[32,256]{1,0:T(8,128)S(1)}) custom-call(bf16[256,256]{1,0:T(8,128)(2,1)} %tf_ref.1, bf16[256,256]{1,0:T(8,128)(2,1)} %sf_ref.1, s32[1,256]{1,0:T(1,128)} %bitcast.2, bf16[256,8192]{1,0:T(8,128)(2,1)} %w_hbm.1), custom_call_target="tpu_custom_call" | custom-call | tf_op jit(solution)/shard_map/sinkhorn/pallas_call | solution.py:346
  83.6 2.1 %write_out.1 = (bf16[256,8192]{1,0:T(8,128)(2,1)}, f32[8,8192]{1,0:T(8,128)}, f32[32,256]{1,0:T(8,128)}) custom-call(bf16[256,8192]{1,0:T(8,128)(2,1)S(1)} %get-tuple-element.9.refs_0_, f32[8,8192]{1,0:T(8,128)S(1)} %get-tuple-element.10.refs_1_, f32[32,256]{1,0:T(8,128)S(1)} %get-tuple-element.11.refs_2_), custom_call_target="tpu_custom_call" | custom-call | tf_op jit(solution)/shard_map/write_out/pallas_call | solution.py:393

commit v4 on v3

v4 whole, which is shorter than its diff:
```python
import math

import jax
import jax.numpy as jnp
from jax import lax
from jax.experimental import pallas as pl
from jax.experimental.pallas import tpu as pltpu
from jax.sharding import PartitionSpec as P

SWEEPS = 3
TEACHER = math.log2(math.e) / 0.07
STUDENT = math.log2(math.e) / 0.1
MESH = pl.DeviceIdType.MESH
NX, NY, NC, NZ = 4, 4, 2, 8
ROWS = 256
WIDE = 1024
BLOCKS = 8
HALF = BLOCKS // 2
TILES = WIDE // 128
PARTS = WIDE // 256
LINE = HALF * TILES // 2
NT = (((1,), (1,)), ((), ()))
ZC = NZ * NC - 1
FIXED = 11
PT, PS, PM, TOTALS, FEATS, RELAY, SCALARS, TOKENS, FEATURE, SPREAD, PHALF = range(FIXED)
ZS = FIXED
XS = ZS + 2 * (SWEEPS + 1)
YS = XS + 2 * SWEEPS
RS = YS + 2 * SWEEPS
GROUPS = RS + PARTS


def wait_all(ref, sem):
    pltpu.make_async_copy(ref, ref, sem).wait()


def to_rows(lanes, width=ROWS):
    return jnp.transpose(jnp.broadcast_to(lanes, (128, width)))


def kernel(
    tf_ref, sf_ref, mask_ref, w_hbm,
    tgt, weight_ref, feature_ref,
    w, expo, rest, soft, peak_b, acc, t_b, r_b, g_b, delta_a, fpt, f_rx,
    wt, eb, qb, gall, sft, dcat, pcol, scal, tall, wp_tx, rs_rx, a_tx, a_rx,
    live_ref, col, x_tx, x_rx, y_tx, y_rx, p_ref,
    z_tx, z_rx, s_tx, s_rx,
    w_sem, send, recv,
):
    dp = lax.axis_index("dp")
    z = lax.axis_index("proto")
    cx, cy, cc = dp // (NY * NC), lax.rem(dp // NC, NY), lax.rem(dp, NC)

    def at(x, y, c):
        return {"dp": (x * NY + y) * NC + c}

    def row_place(n):
        x = lax.rem(cx + n % NX, NX)
        return x, (cc if n < NX else 1 - cc)

    def row_source(n):
        x = lax.rem(cx + NX - n % NX, NX)
        return x, (cc if n < NX else 1 - cc)

    partner = at(cx, cy, 1 - cc)
    row_peers = [at(row_place(n)[0], cy, row_place(n)[1]) for n in range(1, BLOCKS)]
    x_peers = row_peers[: NX - 1]
    y_peers = [at(cx, lax.rem(cy + k, NY), cc) for k in range(1, NY)]
    z_place = [lax.rem(z + k, NZ) for k in range(1, NZ)]
    z_peers = [{"proto": place} for place in z_place]
    zc_peers = z_peers + [partner] + [
        {"dp": dp + 1 - 2 * cc, "proto": place} for place in z_place]

    barrier = pltpu.get_barrier_semaphore()
    peers = row_peers + y_peers + z_peers + zc_peers[NZ:]
    for peer in peers:
        pl.semaphore_signal(barrier, inc=1, device_id=peer, device_id_type=MESH)

    def column(v):
        return pl.multiple_of(lax.rem(cc * HALF + v, BLOCKS) * WIDE, WIDE)

    def load(v):
        return pltpu.make_async_copy(w_hbm.at[:, pl.ds(column(v), WIDE)], w.at[v], w_sem.at[v])

    def start_load(v, c):
        load(v).start()
        return c

    lax.fori_loop(0, BLOCKS, start_load, 0)

    def wait_load(v, c):
        load(v).wait()
        return c

    def send_one(src, dst, group, device):
        pltpu.make_async_remote_copy(
            src_ref=src, dst_ref=dst, send_sem=send.at[group], recv_sem=recv.at[group],
            device_id=device, device_id_type=MESH,
        ).start()

    def push(src, dst, group, devices):
        for k, device in enumerate(devices):
            send_one(src, dst.at[k], group, device)

    def push_z(slot, tc):
        for n in (4, 12, 3, 5, 11, 13, 2, 6, 10, 14, 1, 7, 9, 15, 8):
            send_one(z_tx.at[slot, tc], z_rx.at[slot, tc, n - 1], ZS + 2 * slot + tc,
                     zc_peers[n - 1])

    def wait_z(slot, tc):
        wait_all(z_rx.at[slot, tc], recv.at[ZS + 2 * slot + tc])

    def gather(first, last):
        def piece(q, c):
            for n in range(1, NX):
                at_q = (q // 4, pl.ds(pl.multiple_of(q % 4 * 64, 64), 64))
                send_one(gall.at[(0,) + at_q], gall.at[(n,) + at_q], FEATS, x_peers[n - 1])
            return c

        lax.fori_loop(first, last, piece, 0)

    def logits(feats, table, blocks, first):
        acc[0] = jnp.full(acc.shape[1:], -jnp.inf, jnp.float32)

        def block(v, c):
            if first:
                load(v).wait()
            for s in range(PARTS):
                part = jnp.dot(
                    feats[...], w[v, :, s * 256:(s + 1) * 256],
                    preferred_element_type=jnp.float32,
                )
                table[v, :, s * 256:(s + 1) * 256] = part
                acc[0] = jnp.maximum(acc[0], jnp.maximum(part[:, :128], part[:, 128:]))
            return c

        lax.fori_loop(0, blocks, block, 0)
        peak_b[...] = jnp.broadcast_to(jnp.max(acc[0], axis=1, keepdims=True), peak_b.shape)
        return jnp.max(jnp.transpose(acc[0]), axis=0, keepdims=True)

    def powers(table, scale, blocks, total):
        def block(v, c):
            for s in range(TILES):
                at_s = (v, slice(None), slice(s * 128, (s + 1) * 128))
                value = jnp.exp2((table[at_s] - peak_b[...]) * scale)
                table[at_s] = value
                if total:
                    acc[0] += value
            return c

        lax.fori_loop(0, blocks, block, 0)

    def row_sum(tc):
        return jnp.sum(jnp.transpose(acc[tc]), axis=0, keepdims=True)

    def rest_table():
        def block(v, c):
            for s in range(PARTS):
                part = jnp.dot(
                    tf_ref[...], w[HALF + v, :, s * 256:(s + 1) * 256],
                    preferred_element_type=jnp.float32,
                )
                for h in range(2):
                    rest[v, :, s * 256 + h * 128:s * 256 + (h + 1) * 128] = jnp.exp2(
                        (part[:, h * 128:(h + 1) * 128] - r_b[...]) * TEACHER)
            return c

        lax.fori_loop(0, HALF, block, 0)

    def shared_tables(n, c):
        feats_t = gall[n, 0].astype(jnp.bfloat16)
        feats_s = gall[n, 1].astype(jnp.bfloat16)
        sft[:, pl.ds(pl.multiple_of(n * ROWS, ROWS), ROWS)] = feats_s
        for q in range(PARTS):
            rows = slice(q * 256, (q + 1) * 256)
            dot = jnp.dot(wt[rows, :], feats_t, preferred_element_type=jnp.float32)
            eb[n, rows, :] = jnp.exp2((dot - scal[n, 0:1]) * TEACHER)
            dot = jnp.dot(wt[rows, :], feats_s, preferred_element_type=jnp.float32)
            qb[n, rows, :] = jnp.exp2((dot - scal[n, 1:2]) * STUDENT) * scal[n, 2:3]
        return c

    live = mask_ref[...].astype(jnp.float32)
    live_ref[cc] = live
    own = expo.at[cc]
    others = expo.at[1 - cc]
    z_tx[0, cc] = logits(tf_ref, own, HALF, True)
    gall[0, 0] = jnp.transpose(tf_ref[...].astype(jnp.float32))
    pl.semaphore_wait(barrier, len(peers))
    send_one(gall.at[0, 0], gall.at[NX, 0], PT, partner)
    send_one(live_ref.at[cc], live_ref.at[cc], PM, partner)
    push_z(0, cc)
    powers(own, TEACHER, HALF, False)
    wait_all(gall.at[NX, 0], recv.at[PT])
    delta_a[:, :ROWS] = jnp.transpose(gall[NX, 0].astype(jnp.bfloat16))
    z_tx[0, 1 - cc] = logits(delta_a.at[:, pl.ds(0, ROWS)], others, HALF, False)
    push_z(0, 1 - cc)
    gall[0, 1] = jnp.transpose(sf_ref[...].astype(jnp.float32))
    send_one(gall.at[0, 1], gall.at[NX, 1], PS, partner)
    gather(0, 2)
    powers(others, TEACHER, HALF, False)
    wait_all(live_ref.at[1 - cc], recv.at[PM])

    peaks, factors = [], []
    half_rows = HALF * TILES
    for sweep in range(SWEEPS):
        for tc in range(NC):
            wait_z(sweep, tc)
            if sweep == 0:
                peak = jnp.maximum(jnp.max(z_rx[0, tc], axis=0), z_tx[0, tc])
                peaks.append(peak)
                factors.append(live_ref[tc] * jnp.exp2((z_tx[0, tc] - peak) * TEACHER))
                scale = factors[tc]
            else:
                row = z_tx[sweep, tc] + jnp.sum(z_rx[sweep, tc], axis=0)
                scale = factors[tc] / (row + (1.0 - live_ref[tc]))
            t_b[...] = to_rows(scale)
            for part in range(2):
                def column_block(v, c):
                    for s in range(TILES):
                        r = (v - part * (HALF // 2)) * TILES + s
                        total = jnp.sum(
                            expo[tc, v, :, s * 128:(s + 1) * 128] * t_b[...],
                            axis=0, keepdims=True)
                        if tc:
                            x_tx[sweep, part, pl.ds(r, 1), :] = (
                                col[part, pl.ds(r, 1), :] + total)
                        else:
                            col[part, pl.ds(r, 1), :] = total
                    return c

                lax.fori_loop(part * (HALF // 2), (part + 1) * (HALF // 2), column_block, 0)
                if tc:
                    group = XS + 2 * sweep + part
                    push(x_tx.at[sweep, part], x_rx.at[sweep, part], group, x_peers)

        if sweep == 0:
            lax.fori_loop(HALF, BLOCKS, wait_load, 0)
            student_peak = logits(sf_ref, soft, BLOCKS, False)
        if sweep == 1:
            r_b[...] = to_rows(jnp.where(cc == 0, peaks[0], peaks[1]))
            rest_table()
        if sweep == 2:
            wait_all(gall.at[pl.ds(1, NX - 1)], recv.at[FEATS])
            for n in range(1, NX):
                send_one(gall.at[n], gall.at[NX + n], RELAY, partner)
            lax.fori_loop(0, 3, shared_tables, 0)
        for part in range(2):
            wait_all(x_rx.at[sweep, part], recv.at[XS + 2 * sweep + part])
            y_tx[sweep, part] = x_tx[sweep, part] + jnp.sum(x_rx[sweep, part], axis=0)
            push(y_tx.at[sweep, part], y_rx.at[sweep, part], YS + 2 * sweep + part, y_peers)
        if sweep == 0:
            gather(2, 5)
            acc[0] = jnp.zeros(acc.shape[1:], jnp.float32)
            powers(soft, STUDENT, BLOCKS, True)
            student_total = row_sum(0)
            s_tx[0:1] = student_peak
            s_tx[1:2] = student_total
            push(s_tx, s_rx, TOTALS, z_peers)
        if sweep == 1:
            gather(5, 8)
        if sweep == 2:
            lax.fori_loop(3, 5, shared_tables, 0)
        acc[...] = jnp.zeros(acc.shape, jnp.float32)
        for part in range(2):
            wait_all(y_rx.at[sweep, part], recv.at[YS + 2 * sweep + part])
            p_ref[part * LINE:(part + 1) * LINE] = 1.0 / (
                y_tx[sweep, part] + jnp.sum(y_rx[sweep, part], axis=0))
            if part and sweep == SWEEPS - 1:
                send_one(p_ref.at[pl.ds(0, half_rows)], p_ref.at[pl.ds(half_rows, half_rows)],
                         PHALF, partner)
            for tc in range(NC):
                def row_block(v, c):
                    total = acc[tc]
                    for s in range(TILES):
                        total += (expo[tc, v, :, s * 128:(s + 1) * 128]
                                  * p_ref[pl.ds(v * TILES + s, 1), :])
                    acc[tc] = total
                    return c

                lax.fori_loop(part * (HALF // 2), (part + 1) * (HALF // 2), row_block, 0)
                if part:
                    z_tx[sweep + 1, tc] = row_sum(tc) * factors[tc]
                    push_z(sweep + 1, tc)
        if sweep == 0:
            wt[...] = jnp.transpose(w[cx])
            wait_all(s_rx, recv.at[TOTALS])
            top = jnp.maximum(jnp.max(s_rx[:, 0:1], axis=0), student_peak)
            total = student_total * jnp.exp2((student_peak - top) * STUDENT)
            for k in range(NZ - 1):
                total += s_rx[k, 1:2] * jnp.exp2((s_rx[k, 0:1] - top) * STUDENT)
            share = live * jnp.exp2((student_peak - top) * STUDENT) / total
            g_b[...] = to_rows(share)
            scal[0, 0:1] = jnp.where(cc == 0, peaks[0], peaks[1])
            scal[0, 1:2] = student_peak
            scal[0, 2:3] = share
            for n in range(1, BLOCKS):
                send_one(scal.at[0], scal.at[n], SCALARS, row_peers[n - 1])
        if sweep == 1:
            wait_all(scal.at[pl.ds(1, BLOCKS - 1)], recv.at[SCALARS])
            wait_all(gall.at[NX, 1], recv.at[PS])
        if sweep == SWEEPS - 1:
            wait_all(gall.at[pl.ds(NX + 1, NX - 1)], recv.at[RELAY])
            lax.fori_loop(5, BLOCKS, shared_tables, 0)
            for s in range(TILES):
                pcol[s * 128:(s + 1) * 128, :] = to_rows(
                    p_ref[pl.ds(cx * TILES + s, 1), :], 128)

    wait_z(SWEEPS, cc)
    row = z_tx[SWEEPS, cc] + jnp.sum(z_rx[SWEEPS, cc], axis=0)
    scale = 1.0 / (row + (1.0 - live))
    tall[0] = scale * live
    for n in range(1, BLOCKS):
        send_one(tall.at[0], tall.at[n], TOKENS, row_peers[n - 1])
    wait_z(SWEEPS, 1 - cc)
    t_b[...] = to_rows(scale * jnp.where(cc == 0, factors[0], factors[1]))
    r_b[...] = to_rows(scale * live)
    fpt[...] = jnp.zeros(fpt.shape, jnp.float32)

    def own_block(table, factor, v):
        base = column(v)
        for s in range(TILES):
            lanes = slice(s * 128, (s + 1) * 128)
            target = table[:, lanes] * factor[...] * p_ref[pl.ds(v * TILES + s, 1), :]
            tgt[:, pl.ds(pl.multiple_of(base + s * 128, 128), 128)] = target.astype(jnp.bfloat16)
            delta_a[:, lanes] = (soft[v, :, lanes] * g_b[...] - target).astype(jnp.bfloat16)
        fpt[...] += lax.dot_general(
            w[v], delta_a[...], NT, preferred_element_type=jnp.float32
        ).reshape(fpt.shape)

    def first_half(v, c):
        own_block(own.at[v], t_b, v)
        return c

    def second_half(v, c):
        own_block(rest.at[v], r_b, HALF + v)
        return c

    def shared_part(q, c):
        rows = pl.ds(pl.multiple_of(q * 256, 256), 256)
        for n in range(BLOCKS):
            for h in range(2):
                lanes = slice(h * 128, (h + 1) * 128)
                target = eb[n, rows, lanes] * pcol[rows, :] * tall[n, :, lanes]
                dcat[:, n * ROWS + h * 128:n * ROWS + (h + 1) * 128] = (
                    qb[n, rows, lanes] - target).astype(jnp.bfloat16)
        grad = lax.dot_general(sft[...], dcat[...], NT, preferred_element_type=jnp.float32)
        for x in range(NX):
            for y in range(NY):
                top = (x * NY + y) * 16
                wp_tx[q, y, x * 16:(x + 1) * 16, :] = grad[top:top + 16]
        for k in range(1, NY):
            send_one(wp_tx.at[q, lax.rem(cy + k, NY)], rs_rx.at[q, k - 1], RS + q, y_peers[k - 1])
        return c

    lax.fori_loop(0, HALF, first_half, 0)
    wait_all(tall.at[pl.ds(1, BLOCKS - 1)], recv.at[TOKENS])
    lax.fori_loop(0, PARTS, shared_part, 0)
    wait_all(p_ref.at[pl.ds(half_rows, half_rows)], recv.at[PHALF])
    lax.fori_loop(0, HALF, second_half, 0)
    for k in range(1, NZ):
        send_one(fpt.at[z_place[k - 1]], f_rx.at[k - 1], FEATURE, z_peers[k - 1])

    def collect(q, c):
        wait_all(rs_rx.at[q], recv.at[RS + q])
        grad = wp_tx[q, cy] + jnp.sum(rs_rx[q], axis=0)
        a_tx[q] = grad.reshape(BLOCKS, 8, 256)
        for n in range(1, BLOCKS):
            x, core = row_place(n)
            send_one(a_tx.at[q, x * NC + core], a_rx.at[q, n - 1], SPREAD, row_peers[n - 1])
        return c

    lax.fori_loop(0, PARTS, collect, 0)
    wait_all(f_rx, recv.at[FEATURE])
    feature_ref[...] = fpt[z] + jnp.sum(f_rx[...], axis=0)
    wait_all(a_rx, recv.at[SPREAD])
    for q in range(PARTS):
        for n in range(BLOCKS):
            x, core = row_source(n)
            span = pl.ds(pl.multiple_of((core * HALF + x) * WIDE + q * 256, 256), 256)
            weight_ref[:, span] = a_rx[q, n - 1] if n else a_tx[q, cx * NC + cc]

    wait_all(gall.at[NX, 0], send.at[PT])
    wait_all(gall.at[NX, 1], send.at[PS])
    wait_all(live_ref.at[1 - cc], send.at[PM])
    wait_all(s_rx, send.at[TOTALS])
    wait_all(gall.at[pl.ds(1, NX - 1)], send.at[FEATS])
    wait_all(gall.at[pl.ds(NX + 1, NX - 1)], send.at[RELAY])
    wait_all(scal.at[pl.ds(1, BLOCKS - 1)], send.at[SCALARS])
    wait_all(tall.at[pl.ds(1, BLOCKS - 1)], send.at[TOKENS])
    wait_all(f_rx, send.at[FEATURE])
    wait_all(a_rx, send.at[SPREAD])
    wait_all(p_ref.at[pl.ds(half_rows, half_rows)], send.at[PHALF])
    for slot in range(SWEEPS + 1):
        for tc in range(NC):
            wait_all(z_rx.at[slot, tc], send.at[ZS + 2 * slot + tc])
    for sweep in range(SWEEPS):
        for part in range(2):
            wait_all(x_rx.at[sweep, part], send.at[XS + 2 * sweep + part])
            wait_all(y_rx.at[sweep, part], send.at[YS + 2 * sweep + part])
    for q in range(PARTS):
        wait_all(rs_rx.at[q], send.at[RS + q])


def write_out(*refs):
    sems = refs[6]
    copies = [pltpu.make_async_copy(refs[i], refs[3 + i], sems.at[i]) for i in range(3)]
    for copy in copies:
        copy.start()
    for copy in copies:
        copy.wait()


def on_device(teacher_feats, student_feats, proto_weight, token_mask):
    d, protos = proto_weight.shape
    f32, bf16 = jnp.float32, jnp.bfloat16
    shared = pltpu.VMEM((BLOCKS, WIDE, ROWS), f32)
    rows = pltpu.VMEM((ROWS, 128), f32)
    vmem = pl.BlockSpec(memory_space=pltpu.VMEM)
    hbm = pl.BlockSpec(memory_space=pl.ANY)
    results = pl.pallas_call(
        kernel,
        out_shape=(
            pltpu.VMEM((ROWS, protos), bf16),
            pltpu.VMEM((d // (NX * NY * NC), protos), f32),
            pltpu.VMEM((d // NZ, ROWS), f32),
        ),
        in_specs=[vmem, vmem, vmem, hbm],
        out_specs=(vmem, vmem, vmem),
        scratch_shapes=[
            pltpu.VMEM((BLOCKS, d, WIDE), bf16),
            pltpu.VMEM((NC, HALF, ROWS, WIDE), f32),
            pltpu.VMEM((HALF, ROWS, WIDE), f32),
            pltpu.VMEM((BLOCKS, ROWS, WIDE), f32),
            rows,
            pltpu.VMEM((NC, ROWS, 128), f32),
            rows, rows, rows,
            pltpu.VMEM((ROWS, WIDE), bf16),
            pltpu.VMEM((NZ, d // NZ, ROWS), f32),
            pltpu.VMEM((NZ - 1, d // NZ, ROWS), f32),
            pltpu.VMEM((WIDE, d), bf16),
            shared, shared,
            pltpu.VMEM((BLOCKS, 2, d, ROWS), f32),
            pltpu.VMEM((d, BLOCKS * ROWS), bf16),
            pltpu.VMEM((256, BLOCKS * ROWS), bf16),
            pltpu.VMEM((WIDE, 128), f32),
            pltpu.VMEM((BLOCKS, 3, ROWS), f32),
            pltpu.VMEM((BLOCKS, 1, ROWS), f32),
            pltpu.VMEM((PARTS, NY, d // NY, 256), f32),
            pltpu.VMEM((PARTS, NY - 1, d // NY, 256), f32),
            pltpu.VMEM((PARTS, BLOCKS, 8, 256), f32),
            pltpu.VMEM((PARTS, BLOCKS - 1, 8, 256), f32),
            pltpu.VMEM((NC, 1, ROWS), f32),
            pltpu.VMEM((2, LINE, 128), f32),
            pltpu.VMEM((SWEEPS, 2, LINE, 128), f32),
            pltpu.VMEM((SWEEPS, 2, NX - 1, LINE, 128), f32),
            pltpu.VMEM((SWEEPS, 2, LINE, 128), f32),
            pltpu.VMEM((SWEEPS, 2, NY - 1, LINE, 128), f32),
            pltpu.VMEM((BLOCKS * TILES, 128), f32),
            pltpu.VMEM((SWEEPS + 1, NC, 1, ROWS), f32),
            pltpu.VMEM((SWEEPS + 1, NC, ZC, 1, ROWS), f32),
            pltpu.VMEM((2, ROWS), f32),
            pltpu.VMEM((NZ - 1, 2, ROWS), f32),
            pltpu.SemaphoreType.DMA((BLOCKS,)),
            pltpu.SemaphoreType.DMA((GROUPS,)),
            pltpu.SemaphoreType.DMA((GROUPS,)),
        ],
        compiler_params=pltpu.CompilerParams(
            collective_id=0, has_side_effects=True, vmem_limit_bytes=58 * 2**20
        ),
        name="sinkhorn",
    )(teacher_feats, student_feats, token_mask.reshape(1, -1), proto_weight)
    targets, weight_grad, feature_grad = pl.pallas_call(
        write_out,
        out_shape=tuple(jax.ShapeDtypeStruct(r.shape, r.dtype) for r in results),
        in_specs=[hbm] * 3,
        out_specs=(hbm, hbm, hbm),
        scratch_shapes=[pltpu.SemaphoreType.DMA((3,))],
        compiler_params=pltpu.CompilerParams(vmem_limit_bytes=2**20),
        name="write_out",
    )(*results)
    return targets, weight_grad, feature_grad.T


def solution(mesh):
    placed = (P("dp", None), P("dp", None), P(None, "proto"), P("dp"))
    return jax.shard_map(
        on_device,
        mesh=mesh,
        in_specs=placed,
        out_specs=(P("dp", "proto"), P("dp", "proto"), P("dp", "proto")),
        check_vma=False,
    )
```

time: 85.8 us -> 82.8 us (0.965)
  Pallas kernels: 85 us -> 82.1 us
    pallas_call x1, Pallas kernels: 82.9 us -> 80 us  [on_device(): pl.pallas_call(kernel, out_shape=(pltpu.VMEM((ROWS, protos), bf16), pltpu...]
where the time goes in v4:
time: 82.8 us; the launch traced here: 82.7 us
  Pallas kernels  82.1 us (99%)
    pallas_call x1, Pallas kernels, on_device(): pl.pallas_call(kernel, out_shape=(pltpu.VMEM((ROWS, protos), bf16), pltpu...  80 us
    pallas_call x1, Pallas kernels, on_device(): pl.pallas_call(write_out, out_shape=tuple((jax.ShapeDtypeStruct(r.shape,...  2.11 us

profile of v4, /device:TPU:1, one launch (start us, length us, event | category | flops | bytes accessed | tf_op | source)
XLA Modules:
  0.0 82.7 jit_solution(1790653274973444997)
XLA Ops:
  0.6 80.0 %sinkhorn.1 = (bf16[256,8192]{1,0:T(8,128)(2,1)S(1)}, f32[8,8192]{1,0:T(8,128)S(1)}, f32[32,256]{1,0:T(8,128)S(1)}) custom-call(bf16[256,256]{1,0:T(8,128)(2,1)} %tf_ref.1, bf16[256,256]{1,0:T(8,128)(2,1)} %sf_ref.1, s32[1,256]{1,0:T(1,128)} %bitcast.2, bf16[256,8192]{1,0:T(8,128)(2,1)} %w_hbm.1), custom_call_target="tpu_custom_call" | custom-call | tf_op jit(solution)/shard_map/sinkhorn/pallas_call | solution.py:420
  80.6 2.1 %write_out.1 = (bf16[256,8192]{1,0:T(8,128)(2,1)}, f32[8,8192]{1,0:T(8,128)}, f32[32,256]{1,0:T(8,128)}) custom-call(bf16[256,8192]{1,0:T(8,128)(2,1)S(1)} %get-tuple-element.9.refs_0_, f32[8,8192]{1,0:T(8,128)S(1)} %get-tuple-element.10.refs_1_, f32[32,256]{1,0:T(8,128)S(1)} %get-tuple-element.11.refs_2_), custom_call_target="tpu_custom_call" | custom-call | tf_op jit(solution)/shard_map/write_out/pallas_call | solution.py:472

commit v5 on v4

v5 whole, which is shorter than its diff:
```python
import math

import jax
import jax.numpy as jnp
from jax import lax
from jax.experimental import pallas as pl
from jax.experimental.pallas import tpu as pltpu
from jax.sharding import PartitionSpec as P

SWEEPS = 3
TEACHER = math.log2(math.e) / 0.07
STUDENT = math.log2(math.e) / 0.1
MESH = pl.DeviceIdType.MESH
NX, NY, NC, NZ = 4, 4, 2, 8
ROWS = 256
WIDE = 1024
BLOCKS = 8
HALF = BLOCKS // 2
TILES = WIDE // 128
PARTS = WIDE // 256
THIN = WIDE // 2
SUBS = THIN // 256
SLOTS = 14
TH = ROWS // 2
LINE = HALF * TILES // 2
NT = (((1,), (1,)), ((), ()))
ZC = NZ * NC - 1
FIXED = 20
PT, PS, PM, TOTALS, SCALARS, TOKENS, PHALF, PEAK = range(8)
FEATS, RELAY, FEATURE, SPREAD = 8, 12, 16, 18
ZS = FIXED
XS = ZS + 2 * SWEEPS
YS = XS + 2 * SWEEPS
RS = YS + 2 * SWEEPS
GROUPS = RS + 2 * SUBS


def wait_all(ref, sem):
    pltpu.make_async_copy(ref, ref, sem).wait()


def to_rows(lanes, width=ROWS):
    return jnp.transpose(jnp.broadcast_to(lanes, (128, width)))


def kernel(
    tf_ref, sf_ref, mask_ref, w_hbm,
    tgt, weight_ref, feature_ref,
    w, expo, rest, soft, peak_b, acc, t_b, r_b, g_b, delta_a, fpt, f_rx,
    wt, eb, qb, gall, sft, dcat, pcol, scal, tall, wp_tx, rs_rx, a_tx, a_rx,
    live_ref, k_rx, col, x_tx, x_rx, y_tx, y_rx, p_ref,
    z_tx, z_rx, s_tx, s_rx,
    w_sem, send, recv,
):
    dp = lax.axis_index("dp")
    z = lax.axis_index("proto")
    cx, cy, cc = dp // (NY * NC), lax.rem(dp // NC, NY), lax.rem(dp, NC)

    def at(x, y, c):
        return {"dp": (x * NY + y) * NC + c}

    here = (cx, cy)

    def place(a, n):
        return lax.rem(here[a] + n % NX, NX), (cc if n < NX else 1 - cc)

    def source(a, n):
        return lax.rem(here[a] + NX - n % NX, NX), (cc if n < NX else 1 - cc)

    def peer_of(a, n):
        far, core = place(a, n)
        return at(cx, far, core) if a else at(far, cy, core)

    def slot_of(a, n):
        if a == 0 or n % NX == 0:
            return n
        return n + 7 if n < NX else n + 6

    partner = at(cx, cy, 1 - cc)
    shared_peers = [(slot_of(a, n), peer_of(a, n))
                    for a in range(2) for n in range(1, BLOCKS) if a == 0 or n != NX]
    x_peers = [peer_of(0, k) for k in range(1, NX)]
    y_peers = [peer_of(1, k) for k in range(1, NY)]
    axis_peers = (x_peers, y_peers)
    z_place = [lax.rem(z + k, NZ) for k in range(1, NZ)]
    z_peers = [{"proto": place} for place in z_place]
    zc_peers = z_peers + [partner] + [
        {"dp": dp + 1 - 2 * cc, "proto": place} for place in z_place]

    barrier = pltpu.get_barrier_semaphore()
    peers = [peer for _, peer in shared_peers] + z_peers + zc_peers[NZ:]
    for peer in peers:
        pl.semaphore_signal(barrier, inc=1, device_id=peer, device_id_type=MESH)

    def column(v):
        return pl.multiple_of(lax.rem(cc * HALF + v, BLOCKS) * WIDE, WIDE)

    def load(v):
        return pltpu.make_async_copy(w_hbm.at[:, pl.ds(column(v), WIDE)], w.at[v], w_sem.at[v])

    def start_load(v, c):
        load(v).start()
        return c

    lax.fori_loop(0, BLOCKS, start_load, 0)

    def send_one(src, dst, group, device):
        pltpu.make_async_remote_copy(
            src_ref=src, dst_ref=dst, send_sem=send.at[group], recv_sem=recv.at[group],
            device_id=device, device_id_type=MESH,
        ).start()

    def push(src, dst, group, devices):
        for k, device in enumerate(devices):
            send_one(src, dst.at[k], group, device)

    far_first = (12, 4, 11, 13, 3, 5, 10, 14, 2, 6, 9, 15, 1, 7, 8)

    def push_z(slot, tc):
        for n in far_first:
            send_one(z_tx.at[slot, tc], z_rx.at[slot, tc, n - 1], ZS + 2 * slot + tc,
                     zc_peers[n - 1])

    def wait_z(slot, tc):
        wait_all(z_rx.at[slot, tc], recv.at[ZS + 2 * slot + tc])

    def gather(a, first, last):
        for q in range(first, last):
            rows = pl.ds(q % 4 * 64, 64)
            for n in range(1, NX):
                send_one(gall.at[q // 4, 0, rows], gall.at[q // 4, slot_of(a, n), rows],
                         FEATS + 2 * a + q // 4, axis_peers[a][n - 1])

    def arrivals(a, t, core):
        return gall.at[t, pl.ds(slot_of(a, core * NX + 1), NX - 1)]

    def relay(t):
        for a in range(2):
            wait_all(arrivals(a, t, 0), recv.at[FEATS + 2 * a + t])
            send_one(arrivals(a, t, 0), arrivals(a, t, 1), RELAY + 2 * a + t, partner)

    def logits(feats, table, low, high, first):
        def block(v, c):
            if first:
                load(v).wait()
            part = jnp.dot(feats[...], w[v], preferred_element_type=jnp.float32)
            table[v - low] = part
            most = part[:, :128]
            for s in range(1, TILES):
                most = jnp.maximum(most, part[:, s * 128:(s + 1) * 128])
            acc[0] = jnp.maximum(acc[0], most)
            return c

        lax.fori_loop(low, high, block, 0)

    def no_peak():
        acc[0] = jnp.full(acc.shape[1:], -jnp.inf, jnp.float32)

    def found_peak():
        return jnp.max(jnp.transpose(acc[0]), axis=0, keepdims=True)

    def powers(table, peak, scale, blocks, total):
        def block(v, c):
            for s in range(TILES):
                at_s = (v, slice(None), slice(s * 128, (s + 1) * 128))
                value = jnp.exp2((table[at_s] - peak[...]) * scale)
                table[at_s] = value
                if total:
                    acc[0] += value
            return c

        lax.fori_loop(0, blocks, block, 0)

    def row_sum(tc):
        return jnp.sum(jnp.transpose(acc[tc]), axis=0, keepdims=True)

    def partner_table(feats, peak):
        def block(v, c):
            for s in range(PARTS):
                part = jnp.dot(
                    feats[...], w[v, :, s * 256:(s + 1) * 256],
                    preferred_element_type=jnp.float32,
                )
                for h in range(2):
                    others[v, :, s * 256 + h * 128:s * 256 + (h + 1) * 128] = jnp.exp2(
                        (part[:, h * 128:(h + 1) * 128] - peak[...]) * TEACHER)
            return c

        lax.fori_loop(0, HALF, block, 0)

    def shared_tables(t, places):
        for a in range(2):
            for n in places:
                slot = slot_of(a, n)
                feats = gall[t, slot].astype(jnp.bfloat16)
                if t:
                    sft[a, :, n * ROWS:(n + 1) * ROWS] = feats
                for q in range(SUBS):
                    rows = slice(q * 256, (q + 1) * 256)
                    dot = jnp.dot(wt[a, rows, :], feats, preferred_element_type=jnp.float32)
                    if t:
                        qb[a, n, rows, :] = jnp.exp2(
                            (dot - scal[slot, 1:2]) * STUDENT) * scal[slot, 2:3]
                    else:
                        eb[a, n, rows, :] = jnp.exp2((dot - scal[slot, 0:1]) * TEACHER)

    live = mask_ref[...].astype(jnp.float32)
    own = expo.at[cc]
    others = expo.at[1 - cc]
    gall[0, 0] = jnp.transpose(tf_ref[...].astype(jnp.float32))
    no_peak()
    logits(tf_ref, own, 0, HALF, True)
    logits(tf_ref, rest, HALF, BLOCKS, True)
    local_peak = found_peak()
    live_ref[cc, 0] = live
    live_ref[cc, 1] = local_peak
    pl.semaphore_wait(barrier, len(peers))
    for n in far_first:
        send_one(live_ref.at[cc, 1], k_rx.at[n - 1], PEAK, zc_peers[n - 1])
    send_one(gall.at[0, 0], gall.at[0, NX], PT, partner)
    send_one(live_ref.at[cc], live_ref.at[cc], PM, partner)
    gather(0, 0, 2)
    gather(1, 0, 3)
    r_b[...] = to_rows(local_peak)
    powers(own, r_b, TEACHER, HALF, False)
    wait_all(gall.at[0, NX], recv.at[PT])
    delta_a[:, :ROWS] = jnp.transpose(gall[0, NX].astype(jnp.bfloat16))
    wait_all(live_ref.at[1 - cc], recv.at[PM])
    t_b[...] = to_rows(live_ref[1 - cc, 1])
    partner_table(delta_a.at[:, pl.ds(0, ROWS)], t_b)
    gall[1, 0] = jnp.transpose(sf_ref[...].astype(jnp.float32))
    send_one(gall.at[1, 0], gall.at[1, NX], PS, partner)

    wait_all(k_rx, recv.at[PEAK])
    joint_peak = jnp.maximum(jnp.max(k_rx[:NZ - 1], axis=0), local_peak)
    own_factor = live * jnp.exp2((local_peak - joint_peak) * TEACHER)
    other_factor = live_ref[1 - cc, 0] * jnp.exp2(
        (live_ref[1 - cc, 1] - jnp.max(k_rx[NZ - 1:], axis=0)) * TEACHER)
    factors = [jnp.where(cc == tc, own_factor, other_factor) for tc in range(NC)]
    half_rows = HALF * TILES
    for sweep in range(SWEEPS):
        for tc in range(NC):
            scale = factors[tc]
            if sweep:
                wait_z(sweep - 1, tc)
                row = z_tx[sweep - 1, tc] + jnp.sum(z_rx[sweep - 1, tc], axis=0)
                scale = scale / (row + (1.0 - live_ref[tc, 0]))
            t_b[...] = to_rows(scale)
            for part in range(2):
                def column_block(v, c):
                    for s in range(TILES):
                        r = (v - part * (HALF // 2)) * TILES + s
                        total = jnp.sum(
                            expo[tc, v, :, s * 128:(s + 1) * 128] * t_b[...],
                            axis=0, keepdims=True)
                        if tc:
                            x_tx[sweep, part, pl.ds(r, 1), :] = (
                                col[part, pl.ds(r, 1), :] + total)
                        else:
                            col[part, pl.ds(r, 1), :] = total
                    return c

                lax.fori_loop(part * (HALF // 2), (part + 1) * (HALF // 2), column_block, 0)
                if tc:
                    group = XS + 2 * sweep + part
                    push(x_tx.at[sweep, part], x_rx.at[sweep, part], group, x_peers)

        if sweep == 0:
            no_peak()
            logits(sf_ref, soft, 0, BLOCKS, False)
            student_peak = found_peak()
            peak_b[...] = to_rows(student_peak)
        if sweep == 1:
            powers(rest, r_b, TEACHER, HALF, False)
        if sweep == 2:
            relay(1)
            for a in range(2):
                wait_all(arrivals(a, 0, 1), recv.at[RELAY + 2 * a])
            shared_tables(0, range(NX, BLOCKS))
        for part in range(2):
            wait_all(x_rx.at[sweep, part], recv.at[XS + 2 * sweep + part])
            y_tx[sweep, part] = x_tx[sweep, part] + jnp.sum(x_rx[sweep, part], axis=0)
            push(y_tx.at[sweep, part], y_rx.at[sweep, part], YS + 2 * sweep + part, y_peers)
        if sweep == 0:
            gather(0, 2, 5)
            acc[0] = jnp.zeros(acc.shape[1:], jnp.float32)
            powers(soft, peak_b, STUDENT, BLOCKS, True)
            student_total = row_sum(0)
            s_tx[0:1] = student_peak
            s_tx[1:2] = student_total
            push(s_tx, s_rx, TOTALS, z_peers)
        if sweep == 1:
            gather(0, 5, 8)
            relay(0)
        if sweep == 2:
            shared_tables(1, range(1, NX))
        acc[...] = jnp.zeros(acc.shape, jnp.float32)
        for part in range(2):
            wait_all(y_rx.at[sweep, part], recv.at[YS + 2 * sweep + part])
            p_ref[part * LINE:(part + 1) * LINE] = 1.0 / (
                y_tx[sweep, part] + jnp.sum(y_rx[sweep, part], axis=0))
            if part and sweep == SWEEPS - 1:
                send_one(p_ref.at[pl.ds(0, half_rows)], p_ref.at[pl.ds(half_rows, half_rows)],
                         PHALF, partner)
            for tc in range(NC):
                def row_block(v, c):
                    total = acc[tc]
                    for s in range(TILES):
                        total += (expo[tc, v, :, s * 128:(s + 1) * 128]
                                  * p_ref[pl.ds(v * TILES + s, 1), :])
                    acc[tc] = total
                    return c

                lax.fori_loop(part * (HALF // 2), (part + 1) * (HALF // 2), row_block, 0)
                if part:
                    z_tx[sweep, tc] = row_sum(tc) * factors[tc]
                    push_z(sweep, tc)
        if sweep == 0:
            gather(1, 3, 6)
            for a in range(2):
                lanes = pl.ds(pl.multiple_of(lax.rem(here[a], 2) * THIN, THIN), THIN)
                wt[a] = jnp.transpose(w[2 * a + here[a] // 2, :, lanes])
            wait_all(s_rx, recv.at[TOTALS])
            top = jnp.maximum(jnp.max(s_rx[:, 0:1], axis=0), student_peak)
            total = student_total * jnp.exp2((student_peak - top) * STUDENT)
            for k in range(NZ - 1):
                total += s_rx[k, 1:2] * jnp.exp2((s_rx[k, 0:1] - top) * STUDENT)
            share = live * jnp.exp2((student_peak - top) * STUDENT) / total
            g_b[...] = to_rows(share)
            scal[0, 0:1] = joint_peak
            scal[0, 1:2] = student_peak
            scal[0, 2:3] = share
            for slot, peer in shared_peers:
                send_one(scal.at[0], scal.at[slot], SCALARS, peer)
        if sweep == 1:
            gather(1, 6, 8)
            wait_all(scal.at[pl.ds(1, SLOTS - 1)], recv.at[SCALARS])
            wait_all(gall.at[1, NX], recv.at[PS])
            shared_tables(0, range(NX))
            shared_tables(1, (0, NX))
        if sweep == SWEEPS - 1:
            for a in range(2):
                wait_all(arrivals(a, 1, 1), recv.at[RELAY + 2 * a + 1])
            shared_tables(1, range(NX + 1, BLOCKS))
            for a in range(2):
                for s in range(TILES // 2):
                    line = a * LINE + here[a] * (TILES // 2) + s
                    pcol[a, s * 128:(s + 1) * 128, :] = to_rows(p_ref[pl.ds(line, 1), :], 128)

    scales = []
    for tc in range(NC):
        wait_z(SWEEPS - 1, tc)
        row = z_tx[SWEEPS - 1, tc] + jnp.sum(z_rx[SWEEPS - 1, tc], axis=0)
        scales.append(1.0 / (row + (1.0 - live_ref[tc, 0])))
    own_scale = jnp.where(cc == 0, scales[0], scales[1])
    tall[0, 0] = own_scale * live
    tall[0, 1] = jnp.where(cc == 0, scales[1], scales[0]) * live_ref[1 - cc, 0]
    for k in range(1, NX):
        send_one(tall.at[0], tall.at[k], TOKENS, x_peers[k - 1])
        send_one(tall.at[0], tall.at[NX - 1 + k], TOKENS, y_peers[k - 1])
    t_b[...] = to_rows(own_scale * own_factor)
    fpt[...] = jnp.zeros(fpt.shape, jnp.float32)

    def own_block(table, v, h):
        base = column(v)
        some = pl.ds(h * TH, TH)
        for s in range(TILES):
            lanes = slice(s * 128, (s + 1) * 128)
            target = table[some, lanes] * t_b[some, :] * p_ref[pl.ds(v * TILES + s, 1), :]
            tgt[some, pl.ds(pl.multiple_of(base + s * 128, 128), 128)] = target.astype(jnp.bfloat16)
            delta_a[:TH, lanes] = (
                soft[v, some, lanes] * g_b[some, :] - target).astype(jnp.bfloat16)
        fpt[h] += lax.dot_general(
            w[v], delta_a[:TH, :], NT, preferred_element_type=jnp.float32
        ).reshape(fpt.shape[1:])

    def own_rows(h):
        def first_half(v, c):
            own_block(own.at[v], v, h)
            return c

        def second_half(v, c):
            own_block(rest.at[v], HALF + v, h)
            return c

        lax.fori_loop(0, HALF, first_half, 0)
        if h == 0:
            wait_all(p_ref.at[pl.ds(half_rows, half_rows)], recv.at[PHALF])
        lax.fori_loop(0, HALF, second_half, 0)
        for k in (4, 3, 5, 2, 6, 1, 7):
            send_one(fpt.at[h, z_place[k - 1]], f_rx.at[h, k - 1], FEATURE + h, z_peers[k - 1])

    def shared_part(q, c):
        rows = pl.ds(pl.multiple_of(q * 256, 256), 256)
        for a in range(2):
            for n in range(BLOCKS):
                for h in range(2):
                    lanes = slice(h * 128, (h + 1) * 128)
                    near = n % NX + (a * (NX - 1) if n % NX else 0)
                    target = (eb[a, n, rows, lanes] * pcol[a, rows, :]
                              * tall[near, n // NX, :, lanes])
                    dcat[:, n * ROWS + h * 128:n * ROWS + (h + 1) * 128] = (
                        qb[a, n, rows, lanes] - target).astype(jnp.bfloat16)
            grad = lax.dot_general(sft[a], dcat[...], NT, preferred_element_type=jnp.float32)
            for x in range(NX):
                for y in range(NY):
                    top = (x * NY + y) * 16
                    if a:
                        wp_tx[a, q, x, y * 16:(y + 1) * 16, :] = grad[top:top + 16]
                    else:
                        wp_tx[a, q, y, x * 16:(x + 1) * 16, :] = grad[top:top + 16]
            for k in (2, 1, 3):
                far = lax.rem(here[1 - a] + k, NX)
                send_one(wp_tx.at[a, q, far], rs_rx.at[a, q, k - 1], RS + a * SUBS + q,
                         axis_peers[1 - a][k - 1])
        return c

    own_rows(0)
    wait_all(tall.at[pl.ds(1, NX + NY - 2)], recv.at[TOKENS])
    lax.fori_loop(0, SUBS, shared_part, 0)
    own_rows(1)

    def collect(q, c):
        for a in range(2):
            wait_all(rs_rx.at[a, q], recv.at[RS + a * SUBS + q])
            grad = wp_tx[a, q, here[1 - a]] + jnp.sum(rs_rx[a, q], axis=0)
            a_tx[a, q] = grad.reshape(BLOCKS, 8, 256)
            for n in range(1, BLOCKS):
                far, core = place(a, n)
                send_one(a_tx.at[a, q, far * NC + core], a_rx.at[a, q, n - 1], SPREAD + a,
                         peer_of(a, n))
        return c

    lax.fori_loop(0, SUBS, collect, 0)
    for h in range(2):
        wait_all(f_rx.at[h], recv.at[FEATURE + h])
        feature_ref[:, h * TH:(h + 1) * TH] = fpt[h, z] + jnp.sum(f_rx[h], axis=0)
    for a in range(2):
        wait_all(a_rx.at[a], recv.at[SPREAD + a])
        for q in range(SUBS):
            for n in range(BLOCKS):
                far, core = source(a, n)
                span = pl.ds(pl.multiple_of(
                    core * HALF * WIDE + (a * NX + far) * THIN + q * 256, 256), 256)
                weight_ref[:, span] = a_rx[a, q, n - 1] if n else a_tx[a, q, here[a] * NC + cc]

    wait_all(gall.at[0, NX], send.at[PT])
    wait_all(gall.at[1, NX], send.at[PS])
    wait_all(live_ref.at[1 - cc], send.at[PM])
    wait_all(s_rx, send.at[TOTALS])
    for a in range(2):
        for t in range(2):
            wait_all(arrivals(a, t, 0), send.at[FEATS + 2 * a + t])
            wait_all(arrivals(a, t, 1), send.at[RELAY + 2 * a + t])
        wait_all(a_rx.at[a], send.at[SPREAD + a])
        wait_all(f_rx.at[a], send.at[FEATURE + a])
        for q in range(SUBS):
            wait_all(rs_rx.at[a, q], send.at[RS + a * SUBS + q])
    wait_all(scal.at[pl.ds(1, SLOTS - 1)], send.at[SCALARS])
    wait_all(tall.at[pl.ds(1, NX + NY - 2)], send.at[TOKENS])
    wait_all(k_rx, send.at[PEAK])
    wait_all(p_ref.at[pl.ds(half_rows, half_rows)], send.at[PHALF])
    for slot in range(SWEEPS):
        for tc in range(NC):
            wait_all(z_rx.at[slot, tc], send.at[ZS + 2 * slot + tc])
    for sweep in range(SWEEPS):
        for part in range(2):
            wait_all(x_rx.at[sweep, part], send.at[XS + 2 * sweep + part])
            wait_all(y_rx.at[sweep, part], send.at[YS + 2 * sweep + part])


def write_out(*refs):
    sems = refs[6]
    copies = [pltpu.make_async_copy(refs[i], refs[3 + i], sems.at[i]) for i in range(3)]
    for copy in copies:
        copy.start()
    for copy in copies:
        copy.wait()


def on_device(teacher_feats, student_feats, proto_weight, token_mask):
    d, protos = proto_weight.shape
    f32, bf16 = jnp.float32, jnp.bfloat16
    shared = pltpu.VMEM((2, BLOCKS, THIN, ROWS), f32)
    rows = pltpu.VMEM((ROWS, 128), f32)
    vmem = pl.BlockSpec(memory_space=pltpu.VMEM)
    hbm = pl.BlockSpec(memory_space=pl.ANY)
    results = pl.pallas_call(
        kernel,
        out_shape=(
            pltpu.VMEM((ROWS, protos), bf16),
            pltpu.VMEM((d // (NX * NY * NC), protos), f32),
            pltpu.VMEM((d // NZ, ROWS), f32),
        ),
        in_specs=[vmem, vmem, vmem, hbm],
        out_specs=(vmem, vmem, vmem),
        scratch_shapes=[
            pltpu.VMEM((BLOCKS, d, WIDE), bf16),
            pltpu.VMEM((NC, HALF, ROWS, WIDE), f32),
            pltpu.VMEM((HALF, ROWS, WIDE), f32),
            pltpu.VMEM((BLOCKS, ROWS, WIDE), f32),
            rows,
            pltpu.VMEM((NC, ROWS, 128), f32),
            rows, rows, rows,
            pltpu.VMEM((ROWS, WIDE), bf16),
            pltpu.VMEM((2, NZ, d // NZ, TH), f32),
            pltpu.VMEM((2, NZ - 1, d // NZ, TH), f32),
            pltpu.VMEM((2, THIN, d), bf16),
            shared, shared,
            pltpu.VMEM((2, SLOTS, d, ROWS), f32),
            pltpu.VMEM((2, d, BLOCKS * ROWS), bf16),
            pltpu.VMEM((256, BLOCKS * ROWS), bf16),
            pltpu.VMEM((2, THIN, 128), f32),
            pltpu.VMEM((SLOTS, 3, ROWS), f32),
            pltpu.VMEM((NX + NY - 1, NC, 1, ROWS), f32),
            pltpu.VMEM((2, SUBS, NX, d // NX, 256), f32),
            pltpu.VMEM((2, SUBS, NX - 1, d // NX, 256), f32),
            pltpu.VMEM((2, SUBS, BLOCKS, 8, 256), f32),
            pltpu.VMEM((2, SUBS, BLOCKS - 1, 8, 256), f32),
            pltpu.VMEM((NC, 2, 1, ROWS), f32),
            pltpu.VMEM((ZC, 1, ROWS), f32),
            pltpu.VMEM((2, LINE, 128), f32),
            pltpu.VMEM((SWEEPS, 2, LINE, 128), f32),
            pltpu.VMEM((SWEEPS, 2, NX - 1, LINE, 128), f32),
            pltpu.VMEM((SWEEPS, 2, LINE, 128), f32),
            pltpu.VMEM((SWEEPS, 2, NY - 1, LINE, 128), f32),
            pltpu.VMEM((BLOCKS * TILES, 128), f32),
            pltpu.VMEM((SWEEPS, NC, 1, ROWS), f32),
            pltpu.VMEM((SWEEPS, NC, ZC, 1, ROWS), f32),
            pltpu.VMEM((2, ROWS), f32),
            pltpu.VMEM((NZ - 1, 2, ROWS), f32),
            pltpu.SemaphoreType.DMA((BLOCKS,)),
            pltpu.SemaphoreType.DMA((GROUPS,)),
            pltpu.SemaphoreType.DMA((GROUPS,)),
        ],
        compiler_params=pltpu.CompilerParams(
            collective_id=0, has_side_effects=True, vmem_limit_bytes=58 * 2**20
        ),
        name="sinkhorn",
    )(teacher_feats, student_feats, token_mask.reshape(1, -1), proto_weight)
    targets, weight_grad, feature_grad = pl.pallas_call(
        write_out,
        out_shape=tuple(jax.ShapeDtypeStruct(r.shape, r.dtype) for r in results),
        in_specs=[hbm] * 3,
        out_specs=(hbm, hbm, hbm),
        scratch_shapes=[pltpu.SemaphoreType.DMA((3,))],
        compiler_params=pltpu.CompilerParams(vmem_limit_bytes=2**20),
        name="write_out",
    )(*results)
    return targets, weight_grad, feature_grad.T


def solution(mesh):
    placed = (P("dp", None), P("dp", None), P(None, "proto"), P("dp"))
    return jax.shard_map(
        on_device,
        mesh=mesh,
        in_specs=placed,
        out_specs=(P("dp", "proto"), P("dp", "proto"), P("dp", "proto")),
        check_vma=False,
    )
```

time: 82.8 us -> 75.7 us (0.914)
  Pallas kernels: 82.1 us -> 75 us
    pallas_call x1, Pallas kernels: 80 us -> 72.9 us  [on_device(): pl.pallas_call(kernel, out_shape=(pltpu.VMEM((ROWS, protos), bf16), pltpu...]
where the time goes in v5:
time: 75.7 us; the launch traced here: 75.6 us
  Pallas kernels  75 us (99%)
    pallas_call x1, Pallas kernels, on_device(): pl.pallas_call(kernel, out_shape=(pltpu.VMEM((ROWS, protos), bf16), pltpu...  72.9 us
    pallas_call x1, Pallas kernels, on_device(): pl.pallas_call(write_out, out_shape=tuple((jax.ShapeDtypeStruct(r.shape,...  2.11 us

profile of v5, /device:TPU:1, one launch (start us, length us, event | category | flops | bytes accessed | tf_op | source)
XLA Modules:
  0.0 75.6 jit_solution(15993163517802107004)
XLA Ops:
  0.6 72.9 %sinkhorn.1 = (bf16[256,8192]{1,0:T(8,128)(2,1)S(1)}, f32[8,8192]{1,0:T(8,128)S(1)}, f32[32,256]{1,0:T(8,128)S(1)}) custom-call(bf16[256,256]{1,0:T(8,128)(2,1)} %tf_ref.1, bf16[256,256]{1,0:T(8,128)(2,1)} %sf_ref.1, s32[1,256]{1,0:T(1,128)} %bitcast.2, bf16[256,8192]{1,0:T(8,128)(2,1)} %w_hbm.1), custom_call_target="tpu_custom_call" | custom-call | tf_op jit(solution)/shard_map/sinkhorn/pallas_call | solution.py:488
  73.5 2.1 %write_out.1 = (bf16[256,8192]{1,0:T(8,128)(2,1)}, f32[8,8192]{1,0:T(8,128)}, f32[32,256]{1,0:T(8,128)}) custom-call(bf16[256,8192]{1,0:T(8,128)(2,1)S(1)} %get-tuple-element.9.refs_0_, f32[8,8192]{1,0:T(8,128)S(1)} %get-tuple-element.10.refs_1_, f32[32,256]{1,0:T(8,128)S(1)} %get-tuple-element.11.refs_2_), custom_call_target="tpu_custom_call" | custom-call | tf_op jit(solution)/shard_map/write_out/pallas_call | solution.py:541

commit v6 on v5

--- a/solution.py
+++ b/solution.py
@@ -374,7 +374,7 @@
             w[v], delta_a[:TH, :], NT, preferred_element_type=jnp.float32
         ).reshape(fpt.shape[1:])
 
-    def own_rows(h):
+    def own_rows(h, early):
         def first_half(v, c):
             own_block(own.at[v], v, h)
             return c
@@ -383,7 +383,10 @@
             own_block(rest.at[v], HALF + v, h)
             return c
 
-        lax.fori_loop(0, HALF, first_half, 0)
+        if h or early:
+            lax.fori_loop(0, HALF, first_half, 0)
+        if early:
+            return
         if h == 0:
             wait_all(p_ref.at[pl.ds(half_rows, half_rows)], recv.at[PHALF])
         lax.fori_loop(0, HALF, second_half, 0)
@@ -415,17 +418,18 @@
                          axis_peers[1 - a][k - 1])
         return c
 
-    own_rows(0)
+    own_rows(0, True)
     wait_all(tall.at[pl.ds(1, NX + NY - 2)], recv.at[TOKENS])
     lax.fori_loop(0, SUBS, shared_part, 0)
-    own_rows(1)
+    own_rows(0, False)
+    own_rows(1, False)
 
     def collect(q, c):
         for a in range(2):
             wait_all(rs_rx.at[a, q], recv.at[RS + a * SUBS + q])
             grad = wp_tx[a, q, here[1 - a]] + jnp.sum(rs_rx[a, q], axis=0)
             a_tx[a, q] = grad.reshape(BLOCKS, 8, 256)
-            for n in range(1, BLOCKS):
+            for n in (6, 2, 5, 7, 1, 3, 4):
                 far, core = place(a, n)
                 send_one(a_tx.at[a, q, far * NC + core], a_rx.at[a, q, n - 1], SPREAD + a,
                          peer_of(a, n))

time: 75.7 us -> 75.3 us (level)
  no operation moved by 1% of the time
where the time goes in v6:
time: 75.3 us; the launch traced here: 75.2 us
  Pallas kernels  74.6 us (99%)
    pallas_call x1, Pallas kernels, on_device(): pl.pallas_call(kernel, out_shape=(pltpu.VMEM((ROWS, protos), bf16), pltpu...  72.5 us
    pallas_call x1, Pallas kernels, on_device(): pl.pallas_call(write_out, out_shape=tuple((jax.ShapeDtypeStruct(r.shape,...  2.11 us

profile of v6, /device:TPU:1, one launch (start us, length us, event | category | flops | bytes accessed | tf_op | source)
XLA Modules:
  0.0 75.2 jit_solution(11598593676039818814)
XLA Ops:
  0.6 72.5 %sinkhorn.1 = (bf16[256,8192]{1,0:T(8,128)(2,1)S(1)}, f32[8,8192]{1,0:T(8,128)S(1)}, f32[32,256]{1,0:T(8,128)S(1)}) custom-call(bf16[256,256]{1,0:T(8,128)(2,1)} %tf_ref.1, bf16[256,256]{1,0:T(8,128)(2,1)} %sf_ref.1, s32[1,256]{1,0:T(1,128)} %bitcast.2, bf16[256,8192]{1,0:T(8,128)(2,1)} %w_hbm.1), custom_call_target="tpu_custom_call" | custom-call | tf_op jit(solution)/shard_map/sinkhorn/pallas_call | solution.py:492
  73.1 2.1 %write_out.1 = (bf16[256,8192]{1,0:T(8,128)(2,1)}, f32[8,8192]{1,0:T(8,128)}, f32[32,256]{1,0:T(8,128)}) custom-call(bf16[256,8192]{1,0:T(8,128)(2,1)S(1)} %get-tuple-element.9.refs_0_, f32[8,8192]{1,0:T(8,128)S(1)} %get-tuple-element.10.refs_1_, f32[32,256]{1,0:T(8,128)S(1)} %get-tuple-element.11.refs_2_), custom_call_target="tpu_custom_call" | custom-call | tf_op jit(solution)/shard_map/write_out/pallas_call | solution.py:545
